TPU v7x, 32 devices: a whole 2x2x4 slice. The times are simulated.
32 devices in a mesh: section: 2 (over y), batch: 16 (over z, x, core).
Axes of the slice: x: 2, y: 2, z: 4, core: 2. Of those that a mesh axis runs over, the one named last changes fastest.
Arguments:
- inputs: bfloat16 [2, 32, 256, 768], P('section', 'batch'), may hold values from -6 to 6
- cotangent: bfloat16 [2, 32, 256, 768], P('section', 'batch'), may hold values from -6 to 6
- segments: int32 [2, 32, 256], P(None, 'batch'), may hold values from 0 to 3, never falling along the last dimension, each value on 1 to 128 neighbouring positions
- buckets: int32 [511], replicated, may hold values from 0 to 31
- qkv_weight: bfloat16 [2, 768, 2304], P('section'), may hold values from -0.21875 to 0.21875
- out_weight: bfloat16 [2, 768, 768], P('section'), may hold values from -0.875 to 0.875
- in_weight: bfloat16 [2, 768, 3072], P('section'), may hold values from -0.21875 to 0.21875
- down_weight: bfloat16 [2, 3072, 768], P('section'), may hold values from -0.109375 to 0.109375
- cross_first: bfloat16 [2, 768, 768], P('section'), may hold values from -0.21875 to 0.21875
- cross_second: bfloat16 [2, 768, 768], P('section'), may hold values from -0.625 to 0.625
- vectors: float32 [2, 7, 768], P('section'), may hold values from -1.2 to 1.5, as said below
- ffn_bias: float32 [2, 3072], P('section'), may hold values from -3 to 3
- position_table: float32 [2, 32, 12], P('section'), may hold values from -4 to 4
Outputs:
- outputs: bfloat16 [2, 32, 256, 768], P('section', 'batch')
- input_grad: float32 [2, 32, 256, 768], P('section', 'batch')
- qkv_grad: float32 [2, 768, 2304], P('section', 'batch')
- out_grad: float32 [2, 768, 768], P('section', 'batch')
- in_grad: float32 [2, 768, 3072], P('section', 'batch')
- down_grad: float32 [2, 3072, 768], P('section', 'batch')
- cross_first_grad: float32 [2, 768, 768], P('section', 'batch')
- cross_second_grad: float32 [2, 768, 768], P('section', 'batch')
- vectors_grad: float32 [2, 7, 768], P('section', None, 'batch')
- ffn_bias_grad: float32 [2, 3072], P('section', 'batch')
- table_grad: float32 [2, 32, 12], P('section')
Inputs may be any that keep to these rules, and one draw needn't show every extreme that they name: `segments`: each row numbers its packed sentences 0 to 3 in order, every sentence 1 to 128 tokens long and one exactly 128. `vectors`: gains lie in 0.5 to 1.5.
All inputs are finite; a program needn't handle non-finite values.
Results may differ from a plain program's by a relative error of at most 0.022.
Values may be sent and summed in bfloat16 or wider, within the bound.
No kernel may reach another device: no remote copies, remote signals or barrier semaphores. Data moves between devices by JAX's collectives and lax.ppermute only.
A program may use at most 512 MiB of HBM per device.

v0:
```python
import jax
import jax.numpy as jnp
from jax import lax
from jax.sharding import PartitionSpec as P

MICRO = 2


norm_epsilon = 1e-05
masked_score = -1e30


def passed_along(shard, axis, by):
    devices = lax.axis_size(axis)
    pairs = [(i, i + by) for i in range(devices) if 0 <= i + by < devices]
    return lax.ppermute(shard, axis, pairs)


def layer_norm(values, norm_gain, offset):
    centre = values - jnp.mean(values, axis=-1, keepdims=True)
    spread = jnp.mean(centre * centre, axis=-1, keepdims=True)
    return centre * lax.rsqrt(spread + norm_epsilon) * norm_gain + offset


def gelu_exact(values):
    return jax.nn.gelu(values, approximate=False)


def project(left_side, weight):
    return jnp.einsum("rsd,de->rse", left_side, weight, preferred_element_type=jnp.float32)


def project_back(grad_side, weight):
    return jnp.einsum("rse,de->rsd", grad_side, weight, preferred_element_type=jnp.float32)


def weight_grad(left_side, grad_side):
    return jnp.einsum("rsd,rse->de", left_side, grad_side, preferred_element_type=jnp.float32)


def split_heads(array, heads):
    return array.reshape(array.shape[0], array.shape[1], heads, array.shape[2] // heads)


def score_block(queries, key_rows, position_bias, allowed, heads):
    query_heads = split_heads(queries, heads)
    key_heads = split_heads(key_rows, heads)
    scale = query_heads.shape[3] ** (-0.5)
    raw_scores = jnp.einsum(
        "rqhd,rkhd->rhqk", query_heads, key_heads, preferred_element_type=jnp.float32
    )
    scores = raw_scores * scale + position_bias
    return (jnp.where(allowed[:, None], scores, masked_score), scale)


def attend(queries, key_rows, values, position_bias, allowed, heads):
    scores, scale = score_block(queries, key_rows, position_bias, allowed, heads)
    row_max = jnp.max(scores, axis=-1, keepdims=True)
    exponent = jnp.exp(scores - row_max)
    denominator = jnp.sum(exponent, axis=-1, keepdims=True)
    weights = exponent / denominator
    log_total = row_max + jnp.log(denominator)
    context = jnp.einsum(
        "rhqk,rkhd->rqhd",
        weights.astype(jnp.bfloat16),
        split_heads(values, heads),
        preferred_element_type=jnp.float32,
    )
    return (context.reshape(queries.shape), log_total)


def attend_back(grad_context, queries, key_rows, values, log_total, position_bias, allowed, heads):
    scores, scale = score_block(queries, key_rows, position_bias, allowed, heads)
    weights = jnp.exp(scores - log_total)
    grad_heads = split_heads(grad_context, heads)
    grad_weights = jnp.einsum(
        "rqhd,rkhd->rhqk",
        grad_heads,
        split_heads(values, heads),
        preferred_element_type=jnp.float32,
    )
    centred = jnp.sum(grad_weights * weights, axis=-1, keepdims=True)
    grad_scores = weights * (grad_weights - centred)
    grad_raw = (grad_scores * scale).astype(jnp.bfloat16)
    grad_queries = jnp.einsum(
        "rhqk,rkhd->rqhd",
        grad_raw,
        split_heads(key_rows, heads),
        preferred_element_type=jnp.float32,
    ).reshape(queries.shape)
    grad_keys = jnp.einsum(
        "rhqk,rqhd->rkhd", grad_raw, split_heads(queries, heads), preferred_element_type=jnp.float32
    ).reshape(key_rows.shape)
    grad_values = jnp.einsum(
        "rhqk,rqhd->rkhd",
        weights.astype(jnp.bfloat16),
        grad_heads,
        preferred_element_type=jnp.float32,
    ).reshape(values.shape)
    return (grad_queries, grad_keys, grad_values, jnp.sum(grad_scores, axis=0))


def self_forward(
    residual, qkv_matrix, out_matrix, norm_gain, norm_offset, position_bias, allowed, heads
):
    model_width = residual.shape[2]
    normed = layer_norm(residual, norm_gain, norm_offset).astype(jnp.bfloat16)
    projected = project(normed, qkv_matrix)
    queries = projected[..., :model_width].astype(jnp.bfloat16)
    key_rows = projected[..., model_width : 2 * model_width].astype(jnp.bfloat16)
    values = projected[..., 2 * model_width :].astype(jnp.bfloat16)
    context, log_total = attend(queries, key_rows, values, position_bias, allowed, heads)
    context_low = context.astype(jnp.bfloat16)
    updated = residual + project(context_low, out_matrix)
    return (updated, (residual, normed, queries, key_rows, values, log_total, context_low))


def self_backward(
    grad_out, saved, qkv_matrix, out_matrix, norm_gain, norm_offset, position_bias, allowed, heads
):
    residual, normed, queries, key_rows, values, log_total, context_low = saved
    grad_branch = grad_out.astype(jnp.bfloat16)
    out_grad = weight_grad(context_low, grad_branch)
    grad_context = project_back(grad_branch, out_matrix).astype(jnp.bfloat16)
    grad_queries, grad_keys, grad_values, bias_grad = attend_back(
        grad_context, queries, key_rows, values, log_total, position_bias, allowed, heads
    )
    grad_projected = jnp.concatenate(
        [
            grad_queries.astype(jnp.bfloat16),
            grad_keys.astype(jnp.bfloat16),
            grad_values.astype(jnp.bfloat16),
        ],
        axis=-1,
    )
    qkv_grad = weight_grad(normed, grad_projected)
    grad_normed = project_back(grad_projected, qkv_matrix)
    grad_residual, gain_grad, offset_grad = jax.vjp(layer_norm, residual, norm_gain, norm_offset)[
        1
    ](grad_normed)
    return (grad_out + grad_residual, qkv_grad, out_grad, gain_grad, offset_grad, bias_grad)


def feed_forward(residual, in_matrix, in_bias, down_matrix, down_bias, norm_gain, norm_offset):
    normed = layer_norm(residual, norm_gain, norm_offset).astype(jnp.bfloat16)
    hidden = project(normed, in_matrix) + in_bias
    activated = gelu_exact(hidden).astype(jnp.bfloat16)
    updated = residual + (project(activated, down_matrix) + down_bias)
    return (updated, (residual, normed, hidden, activated))


def feed_backward(grad_out, saved, in_matrix, down_matrix, norm_gain, norm_offset):
    residual, normed, hidden, activated = saved
    grad_branch = grad_out.astype(jnp.bfloat16)
    down_grad = weight_grad(activated, grad_branch)
    down_bias_grad = jnp.sum(grad_branch, axis=(0, 1), dtype=jnp.float32)
    grad_activated = project_back(grad_branch, down_matrix)
    grad_hidden = jax.vjp(gelu_exact, hidden)[1](grad_activated)[0].astype(jnp.bfloat16)
    in_bias_grad = jnp.sum(grad_hidden, axis=(0, 1), dtype=jnp.float32)
    in_grad = weight_grad(normed, grad_hidden)
    grad_normed = project_back(grad_hidden, in_matrix)
    grad_residual, gain_grad, offset_grad = jax.vjp(layer_norm, residual, norm_gain, norm_offset)[
        1
    ](grad_normed)
    return (
        grad_out + grad_residual,
        in_grad,
        in_bias_grad,
        down_grad,
        down_bias_grad,
        gain_grad,
        offset_grad,
    )


def encoder_forward(enc_rows, weights, position_bias, enc_ids, heads):
    (
        qkv_matrix,
        out_matrix,
        in_matrix,
        down_matrix,
        first_matrix,
        second_matrix,
        vector_rows,
        in_bias,
    ) = weights
    allowed = enc_ids[:, :, None] == enc_ids[:, None, :]
    residual = enc_rows.astype(jnp.float32)
    attended, saved_attention = self_forward(
        residual,
        qkv_matrix,
        out_matrix,
        vector_rows[0],
        vector_rows[1],
        position_bias,
        allowed,
        heads,
    )
    mixed, saved_feed = feed_forward(
        attended, in_matrix, in_bias, down_matrix, vector_rows[6], vector_rows[2], vector_rows[3]
    )
    memory = layer_norm(mixed, vector_rows[4], vector_rows[5])
    memory_low = memory.astype(jnp.bfloat16)
    key_rows = project(memory_low, first_matrix).astype(jnp.bfloat16)
    value_rows = project(memory_low, second_matrix).astype(jnp.bfloat16)
    return (memory, key_rows, value_rows, (saved_attention, saved_feed, mixed, memory_low))


def encoder_backward(
    cotangent_rows, grad_keys, grad_values, saved, weights, position_bias, enc_ids, heads
):
    (
        qkv_matrix,
        out_matrix,
        in_matrix,
        down_matrix,
        first_matrix,
        second_matrix,
        vector_rows,
        in_bias,
    ) = weights
    allowed = enc_ids[:, :, None] == enc_ids[:, None, :]
    saved_attention, saved_feed, mixed, memory_low = saved
    first_grad = weight_grad(memory_low, grad_keys)
    second_grad = weight_grad(memory_low, grad_values)
    grad_memory = (
        project_back(grad_keys, first_matrix)
        + project_back(grad_values, second_matrix)
        + cotangent_rows.astype(jnp.float32)
    )
    grad_mixed, final_gain, final_offset = jax.vjp(
        layer_norm, mixed, vector_rows[4], vector_rows[5]
    )[1](grad_memory)
    grad_attended, in_grad, in_bias_grad, down_grad, down_bias_grad, feed_gain, feed_offset = (
        feed_backward(
            grad_mixed, saved_feed, in_matrix, down_matrix, vector_rows[2], vector_rows[3]
        )
    )
    grad_input, qkv_grad, out_grad, self_gain, self_offset, bias_grad = self_backward(
        grad_attended,
        saved_attention,
        qkv_matrix,
        out_matrix,
        vector_rows[0],
        vector_rows[1],
        position_bias,
        allowed,
        heads,
    )
    vector_grad = jnp.stack(
        [self_gain, self_offset, feed_gain, feed_offset, final_gain, final_offset, down_bias_grad]
    )
    return (
        grad_input,
        (
            qkv_grad,
            out_grad,
            in_grad,
            down_grad,
            first_grad,
            second_grad,
            vector_grad,
            in_bias_grad,
        ),
        bias_grad,
    )


def decoder_step(
    dec_rows, cotangent_rows, key_rows, value_rows, weights, position_bias, dec_ids, enc_ids, heads
):
    (
        qkv_matrix,
        out_matrix,
        in_matrix,
        down_matrix,
        first_matrix,
        second_matrix,
        vector_rows,
        in_bias,
    ) = weights
    positions = jnp.arange(dec_rows.shape[1])
    causal = positions[:, None] >= positions[None, :]
    allowed = (dec_ids[:, :, None] == dec_ids[:, None, :]) & causal[None]
    cross_allowed = dec_ids[:, :, None] == enc_ids[:, None, :]
    residual = dec_rows.astype(jnp.float32)
    attended, saved_attention = self_forward(
        residual,
        qkv_matrix,
        out_matrix,
        vector_rows[0],
        vector_rows[1],
        position_bias,
        allowed,
        heads,
    )
    cross_normed = layer_norm(attended, vector_rows[2], vector_rows[3]).astype(jnp.bfloat16)
    cross_queries = project(cross_normed, first_matrix).astype(jnp.bfloat16)
    cross_context, cross_total = attend(
        cross_queries, key_rows, value_rows, 0.0, cross_allowed, heads
    )
    context_low = cross_context.astype(jnp.bfloat16)
    crossed = attended + project(context_low, second_matrix)
    decoded, saved_feed = feed_forward(
        crossed, in_matrix, in_bias, down_matrix, vector_rows[6], vector_rows[4], vector_rows[5]
    )
    grad_crossed, in_grad, in_bias_grad, down_grad, down_bias_grad, feed_gain, feed_offset = (
        feed_backward(
            cotangent_rows.astype(jnp.float32),
            saved_feed,
            in_matrix,
            down_matrix,
            vector_rows[4],
            vector_rows[5],
        )
    )
    grad_branch = grad_crossed.astype(jnp.bfloat16)
    second_grad = weight_grad(context_low, grad_branch)
    grad_context = project_back(grad_branch, second_matrix).astype(jnp.bfloat16)
    grad_queries, grad_keys, grad_values, unused_bias = attend_back(
        grad_context, cross_queries, key_rows, value_rows, cross_total, 0.0, cross_allowed, heads
    )
    grad_queries_low = grad_queries.astype(jnp.bfloat16)
    first_grad = weight_grad(cross_normed, grad_queries_low)
    grad_normed = project_back(grad_queries_low, first_matrix)
    grad_part, cross_gain, cross_offset = jax.vjp(
        layer_norm, attended, vector_rows[2], vector_rows[3]
    )[1](grad_normed)
    grad_attended = grad_crossed + grad_part
    grad_input, qkv_grad, out_grad, self_gain, self_offset, bias_grad = self_backward(
        grad_attended,
        saved_attention,
        qkv_matrix,
        out_matrix,
        vector_rows[0],
        vector_rows[1],
        position_bias,
        allowed,
        heads,
    )
    vector_grad = jnp.stack(
        [self_gain, self_offset, cross_gain, cross_offset, feed_gain, feed_offset, down_bias_grad]
    )
    grads = (
        qkv_grad,
        out_grad,
        in_grad,
        down_grad,
        first_grad,
        second_grad,
        vector_grad,
        in_bias_grad,
    )
    return (
        decoded,
        grad_input,
        grads,
        bias_grad,
        grad_keys.astype(jnp.bfloat16),
        grad_values.astype(jnp.bfloat16),
    )


def spare_branch(function):

    def zeros_only(*operands):
        return jax.tree.map(jnp.zeros_like, function(*operands))

    return zeros_only


def per_device(
    inputs,
    cotangent,
    segments,
    buckets,
    qkv_weight,
    out_weight,
    in_weight,
    down_weight,
    cross_first,
    cross_second,
    vectors,
    ffn_bias,
    position_table,
):
    heads = position_table.shape[2]
    length = inputs.shape[2]
    bucket_count = position_table.shape[1]
    on_encoder = lax.axis_index("section") == 0
    offsets = jnp.arange(length)[None, :] - jnp.arange(length)[:, None] + (length - 1)
    one_hot = (buckets[offsets][:, :, None] == jnp.arange(bucket_count)[None, None, :]).astype(
        jnp.float32
    )
    position_bias = jnp.einsum(
        "ijb,bh->hij", one_hot, position_table[0], precision=lax.Precision.HIGHEST
    )
    weights = (
        qkv_weight[0],
        out_weight[0],
        in_weight[0],
        down_weight[0],
        cross_first[0],
        cross_second[0],
        vectors[0],
        ffn_bias[0],
    )
    per_micro = inputs.shape[1] // MICRO

    def encode_rows(rows_part, enc_part):
        return encoder_forward(rows_part, weights, position_bias, enc_part, heads)

    def decode_rows(rows_part, cotangent_part, key_part, value_part, dec_part, enc_part):
        return decoder_step(
            rows_part,
            cotangent_part,
            key_part,
            value_part,
            weights,
            position_bias,
            dec_part,
            enc_part,
            heads,
        )

    def encode_back(cotangent_part, key_part, value_part, saved, enc_part):
        return encoder_backward(
            cotangent_part, key_part, value_part, saved, weights, position_bias, enc_part, heads
        )

    def pieces(micro):
        first_row = micro * per_micro
        return (
            inputs[0, first_row : first_row + per_micro],
            cotangent[0, first_row : first_row + per_micro],
            segments[0, first_row : first_row + per_micro],
            segments[1, first_row : first_row + per_micro],
        )

    def run_decoder(micro, got_keys, got_values):
        rows_part, cotangent_part, enc_part, dec_part = pieces(micro)
        return lax.cond(
            on_encoder,
            spare_branch(decode_rows),
            decode_rows,
            rows_part,
            cotangent_part,
            got_keys,
            got_values,
            dec_part,
            enc_part,
        )

    def run_backward(micro, ret_keys, ret_values, saved):
        rows_part, cotangent_part, enc_part, dec_part = pieces(micro)
        return lax.cond(
            on_encoder,
            encode_back,
            spare_branch(encode_back),
            cotangent_part,
            ret_keys,
            ret_values,
            saved,
            enc_part,
        )

    memories = [None] * MICRO
    decodes = [None] * MICRO
    enc_grads = [None] * MICRO
    dec_grads = [None] * MICRO
    enc_sets = [None] * MICRO
    dec_sets = [None] * MICRO
    enc_biases = [None] * MICRO
    dec_biases = [None] * MICRO
    kept = [None] * MICRO
    summed = None
    table_grad = jnp.zeros(position_table.shape[1:], jnp.float32)
    sent_rows = None
    sent_grads = None
    for tick in range(MICRO + 2):
        fresh_rows = None
        fresh_grads = None
        if tick < MICRO:
            run_rows_part, run_cotangent_part, run_enc_part, run_dec_part = pieces(tick)
            memory, key_rows, value_rows, saved = lax.cond(
                on_encoder, encode_rows, spare_branch(encode_rows), run_rows_part, run_enc_part
            )
            memories[tick] = memory
            kept[tick] = saved
            fresh_rows = (key_rows, value_rows)
        if tick >= 2:
            earlier = tick - 2
            enc_grads[earlier], enc_sets[earlier], enc_biases[earlier] = run_backward(
                earlier, sent_grads[0], sent_grads[1], kept[earlier]
            )
        if 1 <= tick <= MICRO:
            former = tick - 1
            decoded, dec_grad, dec_weights, dec_bias, back_keys, back_values = run_decoder(
                former, sent_rows[0], sent_rows[1]
            )
            decodes[former] = decoded
            dec_grads[former] = dec_grad
            dec_sets[former] = dec_weights
            dec_biases[former] = dec_bias
            fresh_grads = (back_keys, back_values)
        if fresh_rows is not None:
            sent_rows = passed_along((fresh_rows[0], fresh_rows[1]), "section", 1)
        if fresh_grads is not None:
            sent_grads = passed_along((fresh_grads[0], fresh_grads[1]), "section", -1)
        if tick >= 2:
            finish_micro = tick - 2
            finish_summed = summed
            finish_table_grad = table_grad
            micro_grads = jax.tree.map(jnp.add, enc_sets[finish_micro], dec_sets[finish_micro])
            finish_table_grad = finish_table_grad + jnp.einsum(
                "hij,ijb->bh",
                enc_biases[finish_micro] + dec_biases[finish_micro],
                one_hot,
                precision=lax.Precision.HIGHEST,
            )
            finish_summed = (
                micro_grads
                if finish_summed is None
                else jax.tree.map(jnp.add, finish_summed, micro_grads)
            )
            summed = finish_summed
            table_grad = finish_table_grad
    summed = (
        lax.psum_scatter(summed[0], "batch", scatter_dimension=0, tiled=True),
        lax.psum_scatter(summed[1], "batch", scatter_dimension=0, tiled=True),
        lax.psum_scatter(summed[2], "batch", scatter_dimension=0, tiled=True),
        lax.psum_scatter(summed[3], "batch", scatter_dimension=0, tiled=True),
        lax.psum_scatter(summed[4], "batch", scatter_dimension=0, tiled=True),
        lax.psum_scatter(summed[5], "batch", scatter_dimension=0, tiled=True),
        lax.psum_scatter(summed[6], "batch", scatter_dimension=1, tiled=True),
        lax.psum_scatter(summed[7], "batch", scatter_dimension=0, tiled=True),
    )
    table_total = lax.psum(table_grad, "batch")
    output_parts = [
        (memories[micro] + decodes[micro]).astype(jnp.bfloat16) for micro in range(MICRO)
    ]
    grad_parts = [enc_grads[micro] + dec_grads[micro] for micro in range(MICRO)]
    return (
        jnp.concatenate(output_parts, axis=0)[None],
        jnp.concatenate(grad_parts, axis=0)[None],
        summed[0][None],
        summed[1][None],
        summed[2][None],
        summed[3][None],
        summed[4][None],
        summed[5][None],
        summed[6][None],
        summed[7][None],
        table_total[None],
    )


def solution(mesh):
    return jax.shard_map(
        per_device,
        mesh=mesh,
        in_specs=(
            P("section", "batch", None, None),
            P("section", "batch", None, None),
            P(None, "batch", None),
            P(),
            P("section", None, None),
            P("section", None, None),
            P("section", None, None),
            P("section", None, None),
            P("section", None, None),
            P("section", None, None),
            P("section", None, None),
            P("section", None),
            P("section", None, None),
        ),
        out_specs=(
            P("section", "batch", None, None),
            P("section", "batch", None, None),
            P("section", "batch", None),
            P("section", "batch", None),
            P("section", "batch", None),
            P("section", "batch", None),
            P("section", "batch", None),
            P("section", "batch", None),
            P("section", None, "batch"),
            P("section", "batch"),
            P("section", None, None),
        ),
        check_vma=False,
    )
```

profile of v0, /device:TPU:0, one launch (start us, length us, event | category | flops | bytes accessed | tf_op | source)
XLA Modules:
  0.0 1595.3 jit_solution(518156370573175168)
XLA Ops:
  7.9 408.2 %gather_fusion = s32[65536]{0:T(1024)S(1)} fusion(s32[511]{0:T(512)S(1)} %copy-done, s32[65536]{0:T(1024)S(1)} %broadcast_clamp_fusion), kind=kCustom, calls=%fused_computation | custom fusion | bytes 786432 | tf_op jit(solution)/shard_map/gather | solution.py:392
  421.0 5.0 fusion.442
  426.1 61.4 %conditional.6 = (f32[1,256,768]{2,1,0:T(8,128)}, bf16[1,256,768]{2,1,0:T(8,128)(2,1)}, bf16[1,256,768]{2,1,0:T(8,128)(2,1)}, f32[1,256,768]{2,1,0:T(8,128)}, bf...) conditional(s32[]{:T(128)} %convert_element_type.811, () %tuple.56, ...), branch_computations={%region_0.0_spmd, %region_1.10_spmd} | conditional | flops 4495505408 | bytes 103910848 | solution.py:485
  441.7 5.0 copy.254
  464.9 10.4 fusion.3
  495.4 60.9 %conditional.8 = (f32[1,256,768]{2,1,0:T(8,128)}, bf16[1,256,768]{2,1,0:T(8,128)(2,1)}, bf16[1,256,768]{2,1,0:T(8,128)(2,1)}, f32[1,256,768]{2,1,0:T(8,128)}, bf...) conditional(s32[]{:T(128)} %convert_element_type.811, () %tuple.60, ...), branch_computations={%region_38.0_spmd, %region_39.48_spmd} | conditional | flops 4495505408 | bytes 103914976 | solution.py:485
  510.7 5.0 copy.258
  533.8 10.4 fusion.150
  566.4 28.5 %conditional.7 = (f32[1,256,768]{2,1,0:T(8,128)}, f32[1,256,768]{2,1,0:T(8,128)}, f32[768,2304]{1,0:T(8,128)}, f32[768,768]{1,0:T(8,128)}, f32[768,3072]{1,0:T(8...) conditional(s32[]{:T(128)} %convert_element_type.811, ...), branch_computations={%region_10.37_spmd, %region_37.0_spmd} | conditional | flops 14233312256 | bytes 375349696 | solution.py:442
  570.9 4.9 broadcast.1738
  575.8 4.3 broadcast.1739
  601.3 29.5 %conditional.9 = (f32[1,256,768]{2,1,0:T(8,128)}, f32[1,256,768]{2,1,0:T(8,128)}, f32[768,2304]{1,0:T(8,128)}, f32[768,768]{1,0:T(8,128)}, f32[768,3072]{1,0:T(8...) conditional(s32[]{:T(128)} %convert_element_type.811, ...), branch_computations={%region_48.75_spmd, %region_75.0_spmd} | conditional | flops 14233312256 | bytes 375349696 | solution.py:442
  607.2 4.8 broadcast.1820
  637.2 50.4 %collective-permute-done.4 = bf16[1,256,768]{2,1,0:T(8,128)(2,1)} collective-permute-done((bf16[1,256,768]{2,1,0:T(8,128)(2,1)}, bf16[1,256,768]{2,1,0:T(8,128)(2,1)}, u32[]{:S(2)}, u32[]{:S(2)}) %collective-permute-start.4) | collective-permute-done | bytes 393248 | tf_op jit(solution)/shard_map/ppermute | solution.py:16
  687.6 7.7 collective-permute-done.5
  695.3 162.8 %conditional.10 = (f32[1,256,768]{2,1,0:T(8,128)}, f32[768,768]{0,1:T(8,128)}, f32[768,768]{1,0:T(8,128)}, f32[768,768]{1,0:T(8,128)}, f32[7,768]{1,0:T(8,128)},...) conditional(s32[]{:T(128)} %convert_element_type.811, () %tuple.64, ...), branch_computations={%region_76.0_spmd, %region_77.99_spmd} | conditional | flops 9254606848 | bytes 227667504 | solution.py:456
  706.9 10.8 convert_reduce_fusion.6
  725.5 5.2 fusion.321
  745.9 5.0 copy.266
  751.7 4.8 subtract_exponential_fusion.14
  756.5 6.3 convolution_convert_fusion.18
  762.8 6.3 convolution_convert_fusion.19
  772.6 5.0 convolution_bitcast_fusion.8
  777.6 8.5 copy.315
  786.7 5.3 fusion.322
  805.8 6.5 convolution_bitcast_fusion.7
  812.4 9.6 copy.317
  826.6 6.5 convolution_bitcast_fusion.6
  833.0 9.6 copy.319
  842.6 6.1 subtract_multiply_fusion.2
  858.4 7.7 collective-permute-done.7
  866.0 139.0 %conditional.11 = (f32[1,256,768]{2,1,0:T(8,128)}, f32[768,768]{0,1:T(8,128)S(1)}, f32[768,768]{1,0:T(8,128)}, f32[768,768]{1,0:T(8,128)}, f32[7,768]{1,0:T(8,12...) conditional(s32[]{:T(128)} %convert_element_type.811, () %tuple.66, ...), branch_computations={%region_99.0_spmd, %region_100.122_spmd} | conditional | flops 9254606848 | bytes 227700304 | solution.py:456
  876.8 10.8 convert_reduce_fusion.8
  892.3 5.2 fusion.392
  905.9 5.0 copy.273
  911.0 4.5 subtract_exponential_fusion.15
  915.5 5.5 convolution_convert_fusion.21
  921.1 5.6 convolution_convert_fusion.22
  929.4 5.1 convolution_bitcast_fusion.13
  934.5 8.2 copy.321
  942.8 4.5 fusion.393
  955.2 6.5 convolution_bitcast_fusion.12
  961.8 9.6 copy.323
  973.9 6.5 convolution_bitcast_fusion.11
  980.4 9.6 copy.325
  989.9 5.5 subtract_multiply_fusion.3
  1006.8 5.7 add_add_fusion.23
  1012.6 5.8 add_add_fusion.24
  1023.8 5.9 add_add_fusion.25
  1029.8 13.1 add_add_fusion.22
  1042.9 16.9 %add_add_fusion.20 = f32[3072,768]{1,0:T(8,128)} fusion(f32[3072,768]{1,0:T(8,128)} %get-tuple-element.975, f32[3072,768]{1,0:T(8,128)} %get-tuple-element.454, f32[3072,768]{1,0:T(8,128)} %get-tuple-element.972, f32[3072,768]{1,0:T(8,128)} %get-tuple-element.452), kind=kLoop, calls=%fused_computation.675 | loop fusion | flops 7077888 | bytes 47185920 | tf_op jit(solution)/shard_map/add | solution.py:524
  1060.1 17.4 %add_add_fusion.21 = f32[768,3072]{1,0:T(8,128)} fusion(f32[768,3072]{1,0:T(8,128)} %get-tuple-element.974, f32[768,3072]{1,0:T(8,128)} %get-tuple-element.450, f32[768,3072]{1,0:T(8,128)} %get-tuple-element.971, f32[768,3072]{1,0:T(8,128)} %get-tuple-element.448), kind=kLoop, calls=%fused_computation.676 | loop fusion | flops 7077888 | bytes 47185920 | tf_op jit(solution)/shard_map/add | solution.py:524
  1083.3 5.0 add.741
  1088.3 5.2 copy.284
  1093.5 5.2 add.742
  1098.7 5.3 copy.285
  1105.0 6.4 fusion.443
  1111.4 4.4 fusion.446
  1115.8 60.5 %all-reduce.1 = (f32[3072]{0:T(1024)S(1)}, f32[1,32,12]{1,2,0:T(8,128)S(1)}) all-reduce(f32[3072]{0:T(1024)S(1)} %add_add_fusion.27, f32[1,32,12]{1,2,0:T(8,128)S(1)} %fusion.446), channel_id=9, replica_groups=mesh['section'=2,'batch'=16] {'batch'}, use_global_device_ids=true, to_apply=%region_129.0.clone | all-reduce | flops 3456 | bytes 27648
  1183.2 13.0 reduce-scatter.18.cloned.1.call-done
  1196.2 66.7 %reduce-scatter.12.cloned.1.call-done = f32[48,768]{1,0:T(8,128)} async-done(((f32[768,768]{1,0:T(8,128)}), f32[48,768]{1,0:T(8,128)}) %reduce-scatter.12.cloned.1.call-update) | async-done | bytes 147472 | tf_op jit(solution)/shard_map/reduce_scatter | solution.py:530
  1262.9 93.6 %reduce-scatter.10.cloned.1.call-done = f32[48,2304]{1,0:T(8,128)} async-done(((f32[768,2304]{1,0:T(8,128)}), f32[48,2304]{1,0:T(8,128)}) %reduce-scatter.10.cloned.1.call-update) | async-done | bytes 442384 | tf_op jit(solution)/shard_map/reduce_scatter | solution.py:529
  1356.5 116.0 %reduce-scatter.16.cloned.1.call-done = f32[192,768]{1,0:T(8,128)} async-done(((f32[3072,768]{1,0:T(8,128)}), f32[192,768]{1,0:T(8,128)}) %reduce-scatter.16.cloned.1.call-update) | async-done | bytes 589840 | tf_op jit(solution)/shard_map/reduce_scatter | solution.py:532
  1472.5 115.8 %reduce-scatter.14.cloned.1.call-done = f32[48,3072]{1,0:T(8,128)} async-done(((f32[768,3072]{1,0:T(8,128)}), f32[48,3072]{1,0:T(8,128)}) %reduce-scatter.14.cloned.1.call-update) | async-done | bytes 589840 | tf_op jit(solution)/shard_map/reduce_scatter | solution.py:531
  (384 shorter events, 294.5 us)
Async XLA Ops:
  7.2 1174.6 %reduce-scatter.22.cloned.1.call-start = ((), (), s32[]{:S(2)}) async-start(), calls=%async_computation.13 | async-start | bytes 417792
  7.9 410.5 %copy-start.193 = (s32[2,2,256]{2,1,0:T(2,128)S(1)}, s32[2,2,256]{2,1,0:T(2,128)}, u32[]{:S(2)}) copy-start(s32[2,2,256]{2,1,0:T(2,128)} %param.27) | copy-start | bytes 12292
  7.9 413.2 %copy-start.165 = (f32[1,32,12]{1,0,2:T(1,128)S(1)}, f32[1,32,12]{1,0,2:T(1,128)}, u32[]{:S(2)}) copy-start(f32[1,32,12]{1,0,2:T(1,128)} %param.37) | copy-start | bytes 4612
  416.9 9.2 copy-start.2
  416.9 9.2 copy-start.3
  416.9 9.2 copy-start.6
  419.0 7.1 copy-start.118
  455.0 9.8 slice-start
  455.0 9.8 slice-start.1
  458.5 6.3 copy-start.197
  461.2 14.1 slice-start.8
  464.8 10.5 copy-start.191
  464.8 10.5 slice-start.9
  475.3 5.3 copy-start.149
  475.3 5.3 copy-start.150
  489.4 77.0 %collective-permute-start = (bf16[1,256,768]{1,2,0:T(8,128)(2,1)}, bf16[1,256,768]{1,2,0:T(8,128)(2,1)}, u32[]{:S(2)}, u32[]{:S(2)}) collective-permute-start(bf16[1,256,768]{1,2,0:T(8,128)(2,1)} %copy.255), channel_id=1, source_target_pairs={{0,16},{1,17},{2,18},{3,19},{4,20},{5,21},{6,22},{7,23},{8,24},{9,... | collective-permute-start | bytes 1179656 | tf_op jit(solution)/shard_map/ppermute | solution.py:16
  493.4 73.0 %collective-permute-start.1 = (bf16[1,256,768]{1,2,0:T(8,128)(2,1)}, bf16[1,256,768]{1,2,0:T(8,128)(2,1)}, u32[]{:S(2)}, u32[]{:S(2)}) collective-permute-start(bf16[1,256,768]{1,2,0:T(8,128)(2,1)} %copy.256), channel_id=1, source_target_pairs={{0,16},{1,17},{2,18},{3,19},{4,20},{5,21},{6,22},{7,23},{8,24},{9,... | collective-permute-start | bytes 1179656 | tf_op jit(solution)/shard_map/ppermute | solution.py:16
  510.7 5.0 copy-start.117
  523.9 9.9 slice-start.2
  523.9 9.9 slice-start.3
  527.5 6.3 copy-start.198
  530.2 14.1 slice-start.10
  533.8 10.4 copy-start.192
  533.8 10.4 slice-start.11
  544.2 5.3 copy-start.151
  544.2 5.3 copy-start.152
  558.3 43.0 %collective-permute-start.2 = (bf16[1,256,768]{1,2,0:T(8,128)(2,1)}, bf16[1,256,768]{1,2,0:T(8,128)(2,1)}, u32[]{:S(2)}, u32[]{:S(2)}) collective-permute-start(bf16[1,256,768]{1,2,0:T(8,128)(2,1)} %copy.259), channel_id=1, source_target_pairs={{0,16},{1,17},{2,18},{3,19},{4,20},{5,21},{6,22},{7,23},{8,24},{9,... | collective-permute-start | bytes 1179656 | tf_op jit(solution)/shard_map/ppermute | solution.py:16
  562.3 39.1 %collective-permute-start.3 = (bf16[1,256,768]{1,2,0:T(8,128)(2,1)}, bf16[1,256,768]{1,2,0:T(8,128)(2,1)}, u32[]{:S(2)}, u32[]{:S(2)}) collective-permute-start(bf16[1,256,768]{1,2,0:T(8,128)(2,1)} %copy.260), channel_id=1, source_target_pairs={{0,16},{1,17},{2,18},{3,19},{4,20},{5,21},{6,22},{7,23},{8,24},{9,... | collective-permute-start | bytes 1179656 | tf_op jit(solution)/shard_map/ppermute | solution.py:16
  596.8 90.8 %collective-permute-start.4 = (bf16[1,256,768]{2,1,0:T(8,128)(2,1)}, bf16[1,256,768]{2,1,0:T(8,128)(2,1)}, u32[]{:S(2)}, u32[]{:S(2)}) collective-permute-start(bf16[1,256,768]{2,1,0:T(8,128)(2,1)} %copy.262), channel_id=1, source_target_pairs={{16,0},{17,1},{18,2},{19,3},{20,4},{21,5},{22,6},{23,7},{24,8},{25... | collective-permute-start | bytes 1179656 | tf_op jit(solution)/shard_map/ppermute | solution.py:16
  600.0 95.2 %collective-permute-start.5 = (bf16[1,256,768]{2,1,0:T(8,128)(2,1)}, bf16[1,256,768]{2,1,0:T(8,128)(2,1)}, u32[]{:S(2)}, u32[]{:S(2)}) collective-permute-start(bf16[1,256,768]{2,1,0:T(8,128)(2,1)} %copy.263), channel_id=1, source_target_pairs={{16,0},{17,1},{18,2},{19,3},{20,4},{21,5},{22,6},{23,7},{24,8},{25... | collective-permute-start | bytes 1179656 | tf_op jit(solution)/shard_map/ppermute | solution.py:16
  632.7 225.7 %collective-permute-start.6 = (bf16[1,256,768]{2,1,0:T(8,128)(2,1)}, bf16[1,256,768]{2,1,0:T(8,128)(2,1)}, u32[]{:S(2)}, u32[]{:S(2)}) collective-permute-start(bf16[1,256,768]{2,1,0:T(8,128)(2,1)} %copy.269), channel_id=1, source_target_pairs={{16,0},{17,1},{18,2},{19,3},{20,4},{21,5},{22,6},{23,7},{24,8},{25... | collective-permute-start | bytes 1179656 | tf_op jit(solution)/shard_map/ppermute | solution.py:16
  635.9 230.1 %collective-permute-start.7 = (bf16[1,256,768]{2,1,0:T(8,128)(2,1)}, bf16[1,256,768]{2,1,0:T(8,128)(2,1)}, u32[]{:S(2)}, u32[]{:S(2)}) collective-permute-start(bf16[1,256,768]{2,1,0:T(8,128)(2,1)} %copy.270), channel_id=1, source_target_pairs={{16,0},{17,1},{18,2},{19,3},{20,4},{21,5},{22,6},{23,7},{24,8},{25... | collective-permute-start | bytes 1179656 | tf_op jit(solution)/shard_map/ppermute | solution.py:16
  695.3 170.8 %copy-start.116 = (s32[1,1,256]{2,1,0:T(1,128)S(1)}, s32[1,1,256]{2,1,0:T(1,128)}, u32[]{:S(2)}) copy-start(s32[1,1,256]{2,1,0:T(1,128)} %get-tuple-element.1159) | copy-start | bytes 3076
  699.4 7.5 slice-start.20
  701.1 5.8 slice-start.21
  706.9 10.8 copy-start.66
  725.5 5.3 copy-start.159
  725.5 7.0 copy-start.49
  725.5 7.0 copy-start.182
  786.7 5.3 copy-start.187
  858.1 8.0 copy-start.114
  870.2 6.6 slice-start.22
  871.9 4.9 slice-start.23
  888.8 8.7 copy-start.166
  921.1 8.3 copy-start.95
  926.7 7.8 copy-start.97
  929.3 5.2 copy-start.77
  934.5 8.2 copy-start.171
  942.8 7.7 copy-start.63
  942.8 11.1 copy-start.157
  961.8 9.6 copy-start.172
  961.8 9.6 copy-start.196
  961.8 9.6 copy-start.158
  998.3 6.2 copy-start.41
  1006.8 176.4 %reduce-scatter.20.cloned.1.call-start = ((), (), s32[]{:S(2)}) async-start(), calls=%async_computation.12 | async-start | bytes 2506752 | tf_op jit(solution)/shard_map/reduce_scatter | solution.py:534
  1012.6 183.6 %reduce-scatter.18.cloned.1.call-start = ((), (), s32[]{:S(2)}) async-start(), calls=%async_computation.11 | async-start | bytes 2506752 | tf_op jit(solution)/shard_map/reduce_scatter | solution.py:533
  1018.5 244.4 %reduce-scatter.12.cloned.1.call-start = ((), (), s32[]{:S(2)}) async-start(), calls=%async_computation.8 | async-start | bytes 2506752 | tf_op jit(solution)/shard_map/reduce_scatter | solution.py:530
  1029.7 326.8 %reduce-scatter.10.cloned.1.call-start = ((), (), s32[]{:S(2)}) async-start(), calls=%async_computation.7 | async-start | bytes 7520256 | tf_op jit(solution)/shard_map/reduce_scatter | solution.py:529
  1042.9 429.6 %reduce-scatter.16.cloned.1.call-start = ((), (), s32[]{:S(2)}) async-start(), calls=%async_computation.10 | async-start | bytes 10027008 | tf_op jit(solution)/shard_map/reduce_scatter | solution.py:532
  1059.8 528.4 %reduce-scatter.14.cloned.1.call-start = ((), (), s32[]{:S(2)}) async-start(), calls=%async_computation.9 | async-start | bytes 10027008 | tf_op jit(solution)/shard_map/reduce_scatter | solution.py:531
  1098.7 5.4 copy-start.115
  1098.7 6.2 copy-start.54
  1104.1 7.3 copy-start.21
  1177.6 410.7 %copy-start.1 = (s32[511]{0:T(512)S(1)}, s32[511]{0:T(512)}, u32[]{:S(2)}) copy-start(s32[511]{0:T(512)} %param.28) | copy-start | bytes 6136
  (23 other events, 60.7 us)
Sparse Core Ops, SparseCore 0:
  1006.9 56.0 reduce-scatter.21
  1067.8 61.9 reduce-scatter.19
  1134.1 62.0 reduce-scatter.17
  1200.9 61.9 reduce-scatter.11
  1267.3 89.1 reduce-scatter.9
  1361.6 110.8 reduce-scatter.15
  1477.1 111.1 reduce-scatter.13
where the time goes:
time: 1600 us
  local copies, waits for them, and re-layouts  630 us (39%)
  waiting for transfers between devices  471 us (29%)
  matrix products  240 us (15%)
  other arithmetic  152 us (10%)
  blocking collectives  60.5 us (4%)
    gather x2, local copies, waits for them, and re-layouts, per_device(): buckets[offsets][:, :, None] == jnp.arange(bucket_count)[None, None, :]  409 us
    reduce_scatter x1, waiting for transfers between devices, per_device(): lax.psum_scatter(summed[3], 'batch', scatter_dimension=0, tiled=True)  116 us
    reduce_scatter x1, waiting for transfers between devices, per_device(): lax.psum_scatter(summed[2], 'batch', scatter_dimension=0, tiled=True)  116 us
    reduce_scatter x1, waiting for transfers between devices, per_device(): lax.psum_scatter(summed[0], 'batch', scatter_dimension=0, tiled=True)  93.6 us
    another operation x36, local copies, waits for them, and re-layouts  76.8 us
    reduce_scatter x1, waiting for transfers between devices, per_device(): lax.psum_scatter(summed[1], 'batch', scatter_dimension=0, tiled=True)  66.7 us
    add x8, other arithmetic, per_device(): jax.tree.map(jnp.add, finish_summed, micro_grads)  66.5 us
    ppermute x8, waiting for transfers between devices, passed_along(): return lax.ppermute(shard, axis, pairs)  66 us
  transfers between devices with their start and end apart: 15, of which 9 were waited for; matrix products, arithmetic and copies ran while one was open for 25% of the time, Pallas kernels for 0%

commit v1 on v0

--- a/solution.py
+++ b/solution.py
@@ -3,7 +3,7 @@
 from jax import lax
 from jax.sharding import PartitionSpec as P
 
-MICRO = 2
+MICRO = 1
 
 
 norm_epsilon = 1e-05
@@ -16,6 +16,26 @@
     return lax.ppermute(shard, axis, pairs)
 
 
+def spread_offsets(offset_rows, length):
+    heads = offset_rows.shape[0]
+    turned = jnp.concatenate(
+        [offset_rows[:, length - 1 :], jnp.zeros((heads, 1)), offset_rows[:, : length - 1]], axis=1
+    )
+    period = 2 * length
+    tiled = jnp.broadcast_to(turned[:, None, :], (heads, length, period))
+    flat = tiled.reshape(heads, length * period)[:, : length * (period - 1)]
+    return flat.reshape(heads, length, period - 1)[:, :, :length]
+
+
+def sum_offsets(grid):
+    heads, length = grid.shape[0], grid.shape[1]
+    period = 2 * length
+    padded = jnp.pad(grid, ((0, 0), (0, 0), (0, length - 1)))
+    flat = jnp.pad(padded.reshape(heads, length * (period - 1)), ((0, 0), (0, length)))
+    turned = jnp.sum(flat.reshape(heads, length, period), axis=1)
+    return jnp.concatenate([turned[:, length + 1 :], turned[:, :length]], axis=1)
+
+
 def layer_norm(values, norm_gain, offset):
     centre = values - jnp.mean(values, axis=-1, keepdims=True)
     spread = jnp.mean(centre * centre, axis=-1, keepdims=True)
@@ -36,6 +56,11 @@
 
 def weight_grad(left_side, grad_side):
     return jnp.einsum("rsd,rse->de", left_side, grad_side, preferred_element_type=jnp.float32)
+
+
+def scattered(total):
+    low = lax.psum_scatter(total.astype(jnp.bfloat16), "batch", scatter_dimension=0, tiled=True)
+    return low.astype(jnp.float32)
 
 
 def split_heads(array, heads):
@@ -388,13 +413,11 @@
     length = inputs.shape[2]
     bucket_count = position_table.shape[1]
     on_encoder = lax.axis_index("section") == 0
-    offsets = jnp.arange(length)[None, :] - jnp.arange(length)[:, None] + (length - 1)
-    one_hot = (buckets[offsets][:, :, None] == jnp.arange(bucket_count)[None, None, :]).astype(
-        jnp.float32
-    )
-    position_bias = jnp.einsum(
-        "ijb,bh->hij", one_hot, position_table[0], precision=lax.Precision.HIGHEST
-    )
+    one_hot = (buckets[:, None] == jnp.arange(bucket_count)[None, :]).astype(jnp.float32)
+    offset_bias = jnp.einsum(
+        "ob,bh->ho", one_hot, position_table[0], precision=lax.Precision.HIGHEST
+    )
+    position_bias = spread_offsets(offset_bias, length)
     weights = (
         qkv_weight[0],
         out_weight[0],
@@ -513,8 +536,8 @@
             finish_table_grad = table_grad
             micro_grads = jax.tree.map(jnp.add, enc_sets[finish_micro], dec_sets[finish_micro])
             finish_table_grad = finish_table_grad + jnp.einsum(
-                "hij,ijb->bh",
-                enc_biases[finish_micro] + dec_biases[finish_micro],
+                "ho,ob->bh",
+                sum_offsets(enc_biases[finish_micro] + dec_biases[finish_micro]),
                 one_hot,
                 precision=lax.Precision.HIGHEST,
             )
@@ -526,12 +549,12 @@
             summed = finish_summed
             table_grad = finish_table_grad
     summed = (
-        lax.psum_scatter(summed[0], "batch", scatter_dimension=0, tiled=True),
-        lax.psum_scatter(summed[1], "batch", scatter_dimension=0, tiled=True),
-        lax.psum_scatter(summed[2], "batch", scatter_dimension=0, tiled=True),
-        lax.psum_scatter(summed[3], "batch", scatter_dimension=0, tiled=True),
-        lax.psum_scatter(summed[4], "batch", scatter_dimension=0, tiled=True),
-        lax.psum_scatter(summed[5], "batch", scatter_dimension=0, tiled=True),
+        scattered(summed[0]),
+        scattered(summed[1]),
+        scattered(summed[2]),
+        scattered(summed[3]),
+        scattered(summed[4]),
+        scattered(summed[5]),
         lax.psum_scatter(summed[6], "batch", scatter_dimension=1, tiled=True),
         lax.psum_scatter(summed[7], "batch", scatter_dimension=0, tiled=True),
     )

time: 1600 us -> 1050 us (0.66)
  local copies, waits for them, and re-layouts: 630 us -> 148 us
  waiting for transfers between devices: 471 us -> 576 us
  matrix products: 240 us -> 148 us
  other arithmetic: 152 us -> 82.5 us
    gather x2 -> x0, local copies, waits for them, and re-layouts: 409 us -> none  [per_device(): buckets[offsets][:, :, None] == jnp.arange(bucket_count)[None, None, :]]
    ppermute x8 -> x4, waiting for transfers between devices: 66 us -> 257 us  [passed_along(): return lax.ppermute(shard, axis, pairs)]
    reduce_scatter x6, waiting for transfers between devices: 405 us -> 319 us  [scattered(): lax.psum_scatter(total.astype(jnp.bfloat16), 'batch', scatter_dimension=0...]
    add x12 -> x2, other arithmetic: 69.8 us -> 1.45 us  [per_device(): jax.tree.map(jnp.add, enc_sets[finish_micro], dec_sets[finish_micro])]
    another operation x36 -> x18, local copies, waits for them, and re-layouts: 76.8 us -> 37.2 us
    convert_element_type x2 -> x7, other arithmetic: 3 us -> 38.5 us  [the longest x6 38.2 us: scattered(): total.astype(jnp.bfloat16)]
    cond x8 -> x4, local copies, waits for them, and re-layouts: 60.2 us -> 29.7 us  [run_backward(): lax.cond(on_encoder, encode_back, spare_branch(encode_back), cotangent_pa...]
    dot_general x12 -> x6, matrix products: 54.5 us -> 30.2 us  [weight_grad(): jnp.einsum('rsd,rse->de', left_side, grad_side, preferred_element_type=jn...]
  transfers between devices with their start and end apart: 15 -> 11, of which waited for: 9 -> 9; matrix products, arithmetic and copies ran while one was open for 25% -> 9% of each run, Pallas kernels for 0% -> 0%
where the time goes in v1:
time: 1050 us
  waiting for transfers between devices  576 us (55%)
  matrix products  148 us (14%)
  local copies, waits for them, and re-layouts  148 us (14%)
  other arithmetic  82.5 us (8%)
  blocking collectives  60.4 us (6%)
  between operations  15.1 us (1%)
    reduce_scatter x6, waiting for transfers between devices, scattered(): lax.psum_scatter(total.astype(jnp.bfloat16), 'batch', scatter_dimension=0...  319 us
    ppermute x4, waiting for transfers between devices, passed_along(): return lax.ppermute(shard, axis, pairs)  257 us
    unnamed x1, blocking collectives  60.4 us
    convert_element_type x6, other arithmetic, scattered(): total.astype(jnp.bfloat16)  38.2 us
    another operation x18, local copies, waits for them, and re-layouts  37.2 us
    dot_general x6, matrix products, project(): jnp.einsum('rsd,de->rse', left_side, weight, preferred_element_type=jnp.f...  37 us
    dot_general x6, matrix products, project_back(): jnp.einsum('rse,de->rsd', grad_side, weight, preferred_element_type=jnp.f...  34.3 us
    dot_general x6, matrix products, weight_grad(): jnp.einsum('rsd,rse->de', left_side, grad_side, preferred_element_type=jn...  30.2 us
  transfers between devices with their start and end apart: 11, of which 9 were waited for; matrix products, arithmetic and copies ran while one was open for 9% of the time, Pallas kernels for 0%

profile of v1, /device:TPU:0, one launch (start us, length us, event | category | flops | bytes accessed | tf_op | source)
XLA Modules:
  0.0 1045.1 jit_solution(9457308044054232898)
XLA Ops:
  11.7 4.9 copy.313
  16.5 3.8 slice.120
  20.3 9.3 reshape.435
  29.6 3.8 slice.121
  33.3 67.5 %conditional.3 = (f32[2,256,768]{2,1,0:T(8,128)}, bf16[2,256,768]{2,1,0:T(8,128)(2,1)}, bf16[2,256,768]{2,1,0:T(8,128)(2,1)}, f32[2,256,768]{2,1,0:T(8,128)S(1)}...) conditional(s32[]{:T(128)} %convert_element_type.261, () %tuple.32, ...), branch_computations={%region_0.0_spmd, %region_1.10_spmd} | conditional | flops 9000448000 | bytes 203755040 | solution.py:508
  37.8 3.1 convolution_convert_fusion
  44.7 3.8 copy.256
  51.5 3.5 fusion.18
  56.6 3.1 fusion.23
  63.5 20.2 %fusion.2 = (bf16[2,256,3072]{2,1,0:T(8,128)(2,1)}, f32[2,256,3072]{2,1,0:T(8,128)}) fusion(f32[3072]{0:T(1024)S(1)} %bitcast.382, bf16[2,256,768]{2,1,0:T(8,128)(2,1)} %add_convert_fusion, bf16[768,3072]{1,0:T(8,128)(2,1)S(1)} %bitcast.391), kind=kOutput, calls=%fused_computation.3 | convolution fusion | flops 2519728128 | bytes 14954496 | tf_op jit(solution)/shard_map/cond/branch_1_fun/rsd,de->rse/dot_general | solution.py:50
  83.8 5.7 fusion.223
  91.4 3.2 fusion.215
  94.5 2.9 convolution_convert_fusion.2
  97.5 2.8 convolution_convert_fusion.1
  109.9 12.9 %collective-permute-done = bf16[2,256,768]{1,2,0:T(8,128)(2,1)} collective-permute-done((bf16[2,256,768]{1,2,0:T(8,128)(2,1)}, bf16[2,256,768]{1,2,0:T(8,128)(2,1)}, u32[]{:S(2)}, u32[]{:S(2)}) %collective-permute-start) | collective-permute-done | bytes 786464 | tf_op jit(solution)/shard_map/ppermute | solution.py:16
  122.7 16.6 %collective-permute-done.1 = bf16[2,256,768]{1,2,0:T(8,128)(2,1)} collective-permute-done((bf16[2,256,768]{1,2,0:T(8,128)(2,1)}, bf16[2,256,768]{1,2,0:T(8,128)(2,1)}, u32[]{:S(2)}, u32[]{:S(2)}) %collective-permute-start.1) | collective-permute-done | bytes 786464 | tf_op jit(solution)/shard_map/ppermute | solution.py:16
  139.3 29.3 %conditional.4 = (f32[2,256,768]{2,1,0:T(8,128)}, f32[2,256,768]{2,1,0:T(8,128)}, f32[768,2304]{1,0:T(8,128)}, f32[768,768]{1,0:T(8,128)}, f32[768,3072]{1,0:T(8...) conditional(s32[]{:T(128)} %convert_element_type.261, ...), branch_computations={%region_10.38_spmd, %region_38.0_spmd} | conditional | flops 28521615360 | bytes 619346368 | solution.py:465
  147.0 3.3 broadcast.624
  151.9 4.8 broadcast.626
  156.7 4.3 broadcast.627
  175.8 211.4 %collective-permute-done.2 = bf16[2,256,768]{2,1,0:T(8,128)(2,1)} collective-permute-done((bf16[2,256,768]{2,1,0:T(8,128)(2,1)}, bf16[2,256,768]{2,1,0:T(8,128)(2,1)}, u32[]{:S(2)}, u32[]{:S(2)}) %collective-permute-start.2) | collective-permute-done | bytes 786464 | tf_op jit(solution)/shard_map/ppermute | solution.py:16
  387.2 16.0 %collective-permute-done.3 = bf16[2,256,768]{2,1,0:T(8,128)(2,1)} collective-permute-done((bf16[2,256,768]{2,1,0:T(8,128)(2,1)}, bf16[2,256,768]{2,1,0:T(8,128)(2,1)}, u32[]{:S(2)}, u32[]{:S(2)}) %collective-permute-start.3) | collective-permute-done | bytes 786464 | tf_op jit(solution)/shard_map/ppermute | solution.py:16
  403.2 161.3 %conditional.5 = (f32[2,256,768]{2,1,0:T(8,128)}, f32[768,768]{0,1:T(8,128)S(1)}, f32[768,768]{1,0:T(8,128)}, f32[768,768]{1,0:T(8,128)}, f32[7,768]{1,0:T(8,128...) conditional(s32[]{:T(128)} %convert_element_type.261, () %tuple.36, ...), branch_computations={%region_39.0_spmd, %region_40.63_spmd} | conditional | flops 18512760832 | bytes 431649728 | solution.py:479
  407.6 2.3 fusion.58
  410.0 3.1 multiply_reduce_fusion.4
  415.6 20.1 %convert_reduce_fusion = (f32[3072]{0:T(1024)}, bf16[2,256,3072]{2,1,0:T(8,128)(2,1)S(1)}) fusion(f32[2,256,3072]{2,1,0:T(8,128)} %get-tuple-element.136, bf16[2,256,768]{2,1,0:T(8,128)(2,1)S(1)} %get-tuple-element.622, bf16[3072,768]{1,0:T(8,128)(2,1)S(1)} %bitcast.404), kind=kOutput, calls=%fused_computation.70 | convolution fusion | flops 2532307968 | bytes 14954496 | tf_op jit(solution)/shard_map/cond/branch_1_fun/rse,de->rsd/dot_general | solution.py:54
  435.7 3.0 multiply_reduce_fusion.5
  441.8 4.0 copy.264
  449.7 4.3 subtract_exponential_fusion.1
  454.0 2.6 copy-done.1
  462.3 3.7 fusion.230
  466.0 10.9 %convolution_convert_fusion.4 = bf16[2,12,256,64]{2,3,1,0:T(8,128)(2,1)} fusion(bf16[2,256,12,64]{1,3,2,0:T(8,128)(2,1)} %bitcast.343, f32[2,12,256,256]{2,3,1,0:T(8,128)} %copy-done.1, f32[2,12,256,256]{2,3,1,0:T(8,128)} %fusion.230), kind=kOutput, calls=%fused_computation.124 | convolution fusion | flops 209590528 | bytes 14155776 | tf_op jit(solution)/shard_map/cond/branch_1_fun/rhqk,rqhd->rkhd/dot_general | solution.py:116
  479.2 9.8 convolution_convert_fusion.3
  490.1 5.0 multiply_reduce_fusion.8
  497.8 3.4 convolution_bitcast_fusion.5
  501.3 3.7 convolution_bitcast_fusion.4
  505.0 3.6 convolution_bitcast_fusion.3
  509.3 7.8 fusion.224
  517.1 6.3 convolution_bitcast_fusion
  523.4 8.1 copy.305
  531.6 6.2 convolution_bitcast_fusion.2
  537.8 9.8 copy.307
  547.5 7.0 convolution_bitcast_fusion.1
  554.5 9.8 copy.309
  568.3 3.6 add_convert_fusion.15
  572.0 3.6 add_convert_fusion.14
  575.7 3.6 add_convert_fusion.13
  579.4 7.5 add_convert_fusion.12
  587.0 10.3 add_convert_fusion.11
  597.8 9.6 add_convert_fusion.10
  609.3 2.9 fusion.204
  612.2 3.3 add.346
  615.4 2.4 copy.312
  617.8 5.5 pad.8.clone
  623.3 8.6 reshape.436
  631.9 4.0 pad.9
  635.9 4.9 copy.314
  642.6 60.4 %all-reduce.3 = (f32[3072]{0:T(1024)S(1)}, f32[1,32,12]{1,2,0:T(8,128)S(1)}) all-reduce(f32[3072]{0:T(1024)S(1)} %add.345, f32[1,32,12]{1,2,0:T(8,128)S(1)} %convolution_bitcast_fusion.13), channel_id=9, replica_groups=mesh['section'=2,'batch'=16] {'batch'}, use_global_device_ids=true, to_apply=%region_70.0.clone | all-reduce | flops 3456 | bytes 27648
  704.3 3.3 add_bitcast_fusion.1
  710.5 36.3 %reduce-scatter.18.cloned.1.call-done = bf16[48,768]{1,0:T(8,128)(2,1)} async-done(((bf16[768,768]{1,0:T(8,128)(2,1)}), bf16[48,768]{1,0:T(8,128)(2,1)}) %reduce-scatter.18.cloned.1.call-update) | async-done | bytes 73744 | tf_op jit(solution)/shard_map/reduce_scatter | solution.py:62
  748.4 59.4 %reduce-scatter.20.cloned.1.call-done = bf16[48,768]{1,0:T(8,128)(2,1)} async-done(((bf16[768,768]{1,0:T(8,128)(2,1)}), bf16[48,768]{1,0:T(8,128)(2,1)}) %reduce-scatter.20.cloned.1.call-update) | async-done | bytes 73744 | tf_op jit(solution)/shard_map/reduce_scatter | solution.py:62
  809.3 69.7 %reduce-scatter.10.cloned.1.call-done = bf16[48,2304]{1,0:T(8,128)(2,1)} async-done(((bf16[768,2304]{1,0:T(8,128)(2,1)}), bf16[48,2304]{1,0:T(8,128)(2,1)}) %reduce-scatter.10.cloned.1.call-update) | async-done | bytes 221200 | tf_op jit(solution)/shard_map/reduce_scatter | solution.py:62
  880.8 77.0 %reduce-scatter.14.cloned.1.call-done = bf16[48,3072]{1,0:T(8,128)(2,1)} async-done(((bf16[768,3072]{1,0:T(8,128)(2,1)}), bf16[48,3072]{1,0:T(8,128)(2,1)}) %reduce-scatter.14.cloned.1.call-update) | async-done | bytes 294928 | tf_op jit(solution)/shard_map/reduce_scatter | solution.py:62
  959.6 76.7 %reduce-scatter.16.cloned.1.call-done = bf16[192,768]{1,0:T(8,128)(2,1)} async-done(((bf16[3072,768]{1,0:T(8,128)(2,1)}), bf16[192,768]{1,0:T(8,128)(2,1)}) %reduce-scatter.16.cloned.1.call-update) | async-done | bytes 294928 | tf_op jit(solution)/shard_map/reduce_scatter | solution.py:62
  (230 shorter events, 96.7 us)
Async XLA Ops:
  7.2 700.4 %reduce-scatter.22.cloned.1.call-start = ((), (), s32[]{:S(2)}) async-start(), calls=%async_computation.13 | async-start | bytes 417792
  9.8 129.6 %copy-start.76 = (s32[1,2,256]{2,1,0:T(2,128)}, s32[1,2,256]{2,1,0:T(2,128)S(1)}, u32[]{:S(2)}) copy-start(s32[1,2,256]{2,1,0:T(2,128)S(1)} %slice.105) | copy-start | bytes 6148
  29.6 3.8 copy-start.104
  33.3 106.0 %copy-start.120 = (s32[2,2,256]{2,1,0:T(2,128)S(1)}, s32[2,2,256]{2,1,0:T(2,128)}, u32[]{:S(2)}) copy-start(s32[2,2,256]{2,1,0:T(2,128)} %param.21) | copy-start | bytes 12292
  34.7 3.1 copy-start.121
  36.4 23.4 %copy-start.2 = (f32[2,256,768]{2,1,0:T(8,128)}, f32[2,256,768]{2,1,0:T(8,128)S(1)}, u32[]{:S(2)}) copy-start(f32[2,256,768]{2,1,0:T(8,128)S(1)} %get-tuple-element.689) | copy-start | bytes 4718596 | tf_op jit(solution)/shard_map/cond
  51.5 3.6 copy-start.6
  55.0 1.6 copy-start.62
  56.6 3.1 copy-start.49
  59.7 3.8 slice-start
  59.7 3.8 slice-start.1
  61.9 21.9 %copy-start.4 = (f32[2,256,768]{2,1,0:T(8,128)}, f32[2,256,768]{2,1,0:T(8,128)S(1)}, u32[]{:S(2)}) copy-start(f32[2,256,768]{2,1,0:T(8,128)S(1)} %get-tuple-element.696) | copy-start | bytes 4718596 | tf_op jit(solution)/shard_map/cond
  61.9 21.9 %slice-start.6 = ((s8[4718592]{0:T(1024)(128)(4,1)}), s8[4194304]{0:T(1024)(128)(4,1)S(1)}, s32[]{:S(2)}) async-start(s8[4718592]{0:T(1024)(128)(4,1)} %bitcast.399), calls=%async_computation.20 | async-start | bytes 8388608 | tf_op jit(solution)/shard_map/cond
  63.5 20.3 %slice-start.7 = ((s8[4718592]{0:T(1024)(128)(4,1)}), s8[524288]{0:T(1024)(128)(4,1)S(1)}, s32[]{:S(2)}) async-start(s8[4718592]{0:T(1024)(128)(4,1)} %bitcast.399), calls=%async_computation.21 | async-start | bytes 1048576 | tf_op jit(solution)/shard_map/cond
  89.5 5.1 copy-start.53
  89.5 8.0 copy-start.33
  94.5 5.8 copy-start.3
  94.5 5.8 copy-start.5
  100.9 38.5 %copy-start.72 = (f32[2,12,256,1]{2,1,0,3:T(8,128)}, f32[2,12,256,1]{2,1,0,3:T(8,128)S(1)}, u32[]{:S(2)}) copy-start(f32[2,12,256,1]{2,1,0,3:T(8,128)S(1)} %get-tuple-element.215) | copy-start | bytes 73732
  103.2 19.5 %collective-permute-start = (bf16[2,256,768]{1,2,0:T(8,128)(2,1)}, bf16[2,256,768]{1,2,0:T(8,128)(2,1)}, u32[]{:S(2)}, u32[]{:S(2)}) collective-permute-start(bf16[2,256,768]{1,2,0:T(8,128)(2,1)} %copy.257), channel_id=1, source_target_pairs={{0,16},{1,17},{2,18},{3,19},{4,20},{5,21},{6,22},{7,23},{8,24},{9,... | collective-permute-start | bytes 2359304 | tf_op jit(solution)/shard_map/ppermute | solution.py:16
  107.7 31.7 %collective-permute-start.1 = (bf16[2,256,768]{1,2,0:T(8,128)(2,1)}, bf16[2,256,768]{1,2,0:T(8,128)(2,1)}, u32[]{:S(2)}, u32[]{:S(2)}) collective-permute-start(bf16[2,256,768]{1,2,0:T(8,128)(2,1)} %copy.258), channel_id=1, source_target_pairs={{0,16},{1,17},{2,18},{3,19},{4,20},{5,21},{6,22},{7,23},{8,24},{9,... | collective-permute-start | bytes 2359304 | tf_op jit(solution)/shard_map/ppermute | solution.py:16
  168.6 234.6 %copy-start.74 = (f32[7,768]{1,0:T(8,128)}, f32[7,768]{1,0:T(8,128)S(1)}, u32[]{:S(2)}) copy-start(f32[7,768]{1,0:T(8,128)S(1)} %get-tuple-element.238) | copy-start | bytes 64516
  170.9 216.3 %collective-permute-start.2 = (bf16[2,256,768]{2,1,0:T(8,128)(2,1)}, bf16[2,256,768]{2,1,0:T(8,128)(2,1)}, u32[]{:S(2)}, u32[]{:S(2)}) collective-permute-start(bf16[2,256,768]{2,1,0:T(8,128)(2,1)} %copy.260), channel_id=1, source_target_pairs={{16,0},{17,1},{18,2},{19,3},{20,4},{21,5},{22,6},{23,7},{24,8},{25... | collective-permute-start | bytes 2359304 | tf_op jit(solution)/shard_map/ppermute | solution.py:16
  174.5 228.7 %collective-permute-start.3 = (bf16[2,256,768]{2,1,0:T(8,128)(2,1)}, bf16[2,256,768]{2,1,0:T(8,128)(2,1)}, u32[]{:S(2)}, u32[]{:S(2)}) collective-permute-start(bf16[2,256,768]{2,1,0:T(8,128)(2,1)} %copy.261), channel_id=1, source_target_pairs={{16,0},{17,1},{18,2},{19,3},{20,4},{21,5},{22,6},{23,7},{24,8},{25... | collective-permute-start | bytes 2359304 | tf_op jit(solution)/shard_map/ppermute | solution.py:16
  405.6 4.4 copy-start.32
  405.6 4.4 copy-start.35
  410.0 5.6 slice-start.10
  410.0 5.5 slice-start.11
  413.1 22.6 %slice-start.4 = ((s8[4718592]{0:T(1024)(128)(4,1)}), s8[4194304]{0:T(1024)(128)(4,1)S(1)}, s32[]{:S(2)}) async-start(s8[4718592]{0:T(1024)(128)(4,1)} %bitcast.394), calls=%async_computation.18 | async-start | bytes 8388608 | tf_op jit(solution)/shard_map/cond
  415.3 24.0 %copy-start.14 = (f32[2,256,768]{2,1,0:T(8,128)}, f32[2,256,768]{2,1,0:T(8,128)S(1)}, u32[]{:S(2)}) copy-start(f32[2,256,768]{2,1,0:T(8,128)S(1)} %get-tuple-element.626) | copy-start | bytes 4718596 | tf_op jit(solution)/shard_map/cond
  415.5 20.2 %copy-start.38 = (bf16[2,256,768]{2,1,0:T(8,128)(2,1)}, bf16[2,256,768]{2,1,0:T(8,128)(2,1)S(1)}, u32[]{:S(2)}) copy-start(bf16[2,256,768]{2,1,0:T(8,128)(2,1)S(1)} %get-tuple-element.622) | copy-start | bytes 2359300 | tf_op jit(solution)/shard_map/cond
  415.6 20.1 %slice-start.5 = ((s8[4718592]{0:T(1024)(128)(4,1)}), s8[524288]{0:T(1024)(128)(4,1)S(1)}, s32[]{:S(2)}) async-start(s8[4718592]{0:T(1024)(128)(4,1)} %bitcast.394), calls=%async_computation.19 | async-start | bytes 1048576 | tf_op jit(solution)/shard_map/cond
  435.7 3.0 copy-start.124
  438.7 2.0 copy-start.52
  439.3 1.1 copy-start.20
  439.6 1.1 copy-start.44
  441.5 4.3 copy-start.77
  441.8 20.5 %copy-start.16 = (bf16[2,256,768]{1,2,0:T(8,128)(2,1)}, bf16[2,256,768]{1,2,0:T(8,128)(2,1)S(1)}, u32[]{:S(2)}) copy-start(bf16[2,256,768]{1,2,0:T(8,128)(2,1)S(1)} %copy.245) | copy-start | bytes 2359300 | tf_op jit(solution)/shard_map/cond
  441.8 7.9 copy-start.73
  449.7 4.3 copy-start.36
  454.0 2.6 copy-start.1
  462.3 14.6 %copy-start.26 = (bf16[2,256,768]{1,2,0:T(8,128)(2,1)}, bf16[2,256,768]{1,2,0:T(8,128)(2,1)S(1)}, u32[]{:S(2)}) copy-start(bf16[2,256,768]{1,2,0:T(8,128)(2,1)S(1)} %copy.265) | copy-start | bytes 2359300 | tf_op jit(solution)/shard_map/cond
  466.0 13.2 %copy-start.37 = (bf16[2,256,768]{1,2,0:T(8,128)(2,1)S(1)}, bf16[2,256,768]{1,2,0:T(8,128)(2,1)}, u32[]{:S(2)}) copy-start(bf16[2,256,768]{1,2,0:T(8,128)(2,1)} %copy-done.36) | copy-start | bytes 2359300 | tf_op jit(solution)/shard_map/cond
  490.1 5.8 copy-start.15
  490.1 5.8 copy-start.21
  495.9 1.9 copy-start.45
  501.3 8.1 copy-start.17
  501.3 8.1 copy-start.27
  509.3 7.8 copy-start.57
  509.3 7.8 copy-start.58
  523.4 8.2 copy-start.125
  537.8 9.8 copy-start.39
  554.5 9.8 copy-start.28
  564.5 2.0 copy-start.75
  568.3 140.7 %reduce-scatter.12.cloned.1.call-start = ((), (), s32[]{:S(2)}) async-start(), calls=%async_computation.8 | async-start | bytes 1253376 | tf_op jit(solution)/shard_map/reduce_scatter | solution.py:62
  572.0 174.8 %reduce-scatter.18.cloned.1.call-start = ((), (), s32[]{:S(2)}) async-start(), calls=%async_computation.11 | async-start | bytes 1253376 | tf_op jit(solution)/shard_map/reduce_scatter | solution.py:62
  575.6 232.2 %reduce-scatter.20.cloned.1.call-start = ((), (), s32[]{:S(2)}) async-start(), calls=%async_computation.12 | async-start | bytes 1253376 | tf_op jit(solution)/shard_map/reduce_scatter | solution.py:62
  579.4 299.7 %reduce-scatter.10.cloned.1.call-start = ((), (), s32[]{:S(2)}) async-start(), calls=%async_computation.7 | async-start | bytes 3760128 | tf_op jit(solution)/shard_map/reduce_scatter | solution.py:62
  586.9 370.9 %reduce-scatter.14.cloned.1.call-start = ((), (), s32[]{:S(2)}) async-start(), calls=%async_computation.9 | async-start | bytes 5013504 | tf_op jit(solution)/shard_map/reduce_scatter | solution.py:62
  597.3 439.0 %reduce-scatter.16.cloned.1.call-start = ((), (), s32[]{:S(2)}) async-start(), calls=%async_computation.10 | async-start | bytes 5013504 | tf_op jit(solution)/shard_map/reduce_scatter | solution.py:62
  607.4 0.7 copy-start.123
  640.8 0.8 copy-start.107
  640.8 1.5 copy-start.122
Sparse Core Ops, SparseCore 0:
  568.4 56.0 reduce-scatter.21
  628.6 57.0 reduce-scatter.11
  689.7 57.0 reduce-scatter.17
  750.7 57.0 reduce-scatter.19
  812.0 66.9 reduce-scatter.9
  883.3 74.5 reduce-scatter.13
  961.7 74.5 reduce-scatter.15

commit v2 on v0

v2 whole, which is shorter than its diff:
```python
import functools

import jax
import jax.numpy as jnp
from jax import lax
from jax.experimental import pallas as pl
from jax.experimental.pallas import tpu as pltpu
from jax.sharding import PartitionSpec as P

norm_epsilon = 1e-05
masked_score = -1e30
half_root = 0.7071067811865476
density_scale = 0.3989422804014327
tile = 256
chunk = 64
vmem_bytes = 62 * 1024 * 1024

f32 = jnp.float32
bf16 = jnp.bfloat16
ANY = pl.BlockSpec(memory_space=pl.ANY)
SMEM = pl.BlockSpec(memory_space=pltpu.SMEM)
VMEM = pl.BlockSpec(memory_space=pltpu.VMEM)


def mm(left, right):
    return jnp.dot(left, right, preferred_element_type=f32)


def mm_nt(left, right):
    return lax.dot_general(left, right, (((1,), (1,)), ((), ())), preferred_element_type=f32)


def mm_tn(left, right):
    return lax.dot_general(left, right, (((0,), (0,)), ((), ())), preferred_element_type=f32)


def mean_of(values):
    return jnp.sum(values, axis=-1, keepdims=True) * (1.0 / values.shape[-1])


def normalised(values):
    centre = values - mean_of(values)
    rate = lax.rsqrt(mean_of(centre * centre) + norm_epsilon)
    return centre * rate, rate


def each_rows(count, body):
    @pl.loop(0, count // chunk)
    def _(step):
        body(pl.ds(pl.multiple_of(step * chunk, chunk), chunk))


def each_tile(count, body, width=tile):
    @pl.loop(0, count // width)
    def _(step):
        body(pl.ds(pl.multiple_of(step * width, width), width))


def norm_forward(source, gain, offset, target, also=None):
    def rows(at):
        unit, _ = normalised(source[at, :].astype(f32))
        normed = unit * gain + offset
        target[at, :] = normed.astype(target.dtype)

    each_rows(source.shape[0], rows)


def norm_backward(source, grad_normed, gain, upstream, target, gain_sum, offset_sum):
    gain_sum[...] = jnp.zeros_like(gain_sum)
    offset_sum[...] = jnp.zeros_like(offset_sum)

    def rows(at):
        unit, rate = normalised(source[at, :].astype(f32))
        upper = grad_normed[at, :]
        product = upper * unit
        gain_sum[...] += jnp.sum(product.reshape(-1, 8, product.shape[1]), axis=0)
        offset_sum[...] += jnp.sum(upper.reshape(-1, 8, upper.shape[1]), axis=0)
        scaled = upper * gain
        inner = mean_of(scaled)
        along = mean_of(product * gain)
        result = rate * (scaled - inner - unit * along)
        if upstream is not None:
            result = result + upstream[at, :].astype(f32)
        target[at, :] = result

    each_rows(source.shape[0], rows)


def column_sum(partial):
    return jnp.sum(partial[...], axis=0, keepdims=True)


def lower_lanes(shape):
    return lax.broadcasted_iota(jnp.int32, shape, 1) < shape[1] // 2


def split_pair(block):
    lower = lower_lanes(block.shape)
    zero = jnp.zeros_like(block)
    return jnp.concatenate([jnp.where(lower, block, zero), jnp.where(lower, zero, block)], axis=0)


def join_pair(stacked):
    rows = stacked.shape[0] // 2
    lower = lower_lanes((rows, stacked.shape[1]))
    return jnp.where(lower, stacked[:rows], stacked[rows:])


def attend_pair(queries, key_rows, values, additions, scale):
    length = queries.shape[0]
    scores = mm_nt(queries, split_pair(key_rows)) * scale
    parts = []
    for head in range(2):
        part = scores[:, head * length : (head + 1) * length] + additions[head]
        exponent = jnp.exp(part - jnp.max(part, axis=-1, keepdims=True))
        parts.append(exponent * (1.0 / jnp.sum(exponent, axis=-1, keepdims=True)))
    weights = jnp.concatenate(parts, axis=1).astype(bf16)
    return weights, mm(weights, split_pair(values))


def attend_pair_back(weights, queries, key_rows, values, grad_context, scale):
    length = queries.shape[0]
    grad_weights = mm_nt(grad_context, split_pair(values))
    parts = []
    for head in range(2):
        at = slice(head * length, (head + 1) * length)
        weight = weights[:, at].astype(f32)
        grad_weight = grad_weights[:, at]
        centred = jnp.sum(grad_weight * weight, axis=-1, keepdims=True)
        parts.append(weight * (grad_weight - centred))
    grad_raw = (jnp.concatenate(parts, axis=1) * scale).astype(bf16)
    grad_queries = mm(grad_raw, split_pair(key_rows))
    grad_keys = join_pair(mm_tn(grad_raw, queries))
    grad_values = join_pair(mm_tn(weights, grad_context))
    return grad_queries, grad_keys, grad_values, parts


def same_sentence(query_ids, key_ids):
    length = query_ids.shape[1]
    across = jnp.broadcast_to(key_ids.astype(f32), (length, length))
    down = jnp.broadcast_to(query_ids.astype(f32), (length, length)).T
    return across == down


class Mover:
    def __init__(self, semaphores):
        self.semaphores = semaphores
        self.used = 0

    def start(self, source, target):
        copy = pltpu.make_async_copy(source, target, self.semaphores.at[self.used])
        self.used += 1
        copy.start()
        return copy


def wait_all(copies):
    for copy in copies:
        copy.wait()


def gelu_parts(hidden):
    share = 0.5 + 0.5 * lax.erf(hidden * half_root)
    slope = share + hidden * (density_scale * jnp.exp(hidden * hidden * -0.5))
    return hidden * share, slope


def first_body(
    heads, flag, ids, turned, table, vectors, in_bias, rows_in, cot_in, qkv_in, out_in, ffn_in,
    down_in, first_in,
    x1_out, h1_out, qkv_out, weights_out, context_out, h2_out, u_out, slope_out, e2_out, low_out,
    hc_out, qc_out,
    rows, qkv_w, out_w, ffn_w, down_w, first_w, cot, normed, qkv, weights, context, x1, h2, u, slope,
    e2, low, bias_rows, mask, loads, stores,
):
    width = rows.shape[1]
    hidden_width = ffn_w.shape[1]
    row_count, length = ids.shape[1], ids.shape[2]
    on_encoder = flag[0] == 1
    load = Mover(loads)
    store = Mover(stores)
    got_rows = load.start(rows_in, rows)
    got_qkv = load.start(qkv_in, qkv_w)
    got_out = load.start(out_in, out_w)

    one_hot = (turned[...] == lax.broadcasted_iota(jnp.int32, (table.shape[0], 2 * length), 0)).astype(f32)
    bias_rows[...] = lax.dot_general(
        table[...], one_hot, (((0,), (0,)), ((), ())), precision=lax.Precision.HIGHEST,
        preferred_element_type=f32,
    )
    own_group = jnp.where(on_encoder, 0, 1)
    ahead = lax.broadcasted_iota(jnp.int32, (length, length), 0) >= lax.broadcasted_iota(
        jnp.int32, (length, length), 1
    )
    for row in range(row_count):
        own = ids[pl.ds(own_group, 1), row, :]
        allowed = same_sentence(own, own) & (ahead | on_encoder)
        mask[row] = jnp.where(allowed, 0.0, masked_score)

    got_rows.wait()
    norm_forward(rows, vectors[0:1, :], vectors[1:2, :], normed)
    got_qkv.wait()

    def project(at):
        qkv[:, at] = mm(normed[...], qkv_w[:, at]).astype(bf16)

    each_tile(3 * width, project)
    out_copies = [store.start(normed, h1_out), store.start(qkv, qkv_out)]
    scale = (width // heads) ** (-0.5)

    @pl.loop(0, heads // 2)
    def _(pair):
        lanes = pl.multiple_of(pair * 128, 128)
        biases = []
        for head in range(2):
            spread = jnp.broadcast_to(bias_rows[pl.ds(pair * 2 + head, 1), :], (length, 2 * length))
            skewed = pltpu.roll(spread, 0, 1, stride=1, stride_axis=0)
            biases.append(skewed[:, :length])
        for row in range(row_count):
            at = slice(row * length, (row + 1) * length)
            additions = [bias + mask[row] for bias in biases]
            part, mixed = attend_pair(
                qkv[at, pl.ds(lanes, 128)],
                qkv[at, pl.ds(width + lanes, 128)],
                qkv[at, pl.ds(2 * width + lanes, 128)],
                additions,
                scale,
            )
            weights[row, pair] = part
            context[at, pl.ds(lanes, 128)] = mixed.astype(bf16)

    out_copies += [store.start(weights, weights_out), store.start(context, context_out)]
    got_out.wait()

    def mix(at):
        x1[:, at] = rows[:, at].astype(f32) + mm(context[...], out_w[:, at])

    each_tile(width, mix)
    out_copies.append(store.start(x1, x1_out))

    @pl.when(on_encoder)
    def _():
        got_ffn = load.start(ffn_in, ffn_w)
        got_down = load.start(down_in, down_w)
        norm_forward(x1, vectors[2:3, :], vectors[3:4, :], h2)
        got_ffn.wait()

        def feed(at):
            value, rate = gelu_parts(mm(h2[...], ffn_w[:, at]) + in_bias[:, at])
            u[:, at] = value.astype(bf16)
            slope[:, at] = rate.astype(bf16)

        each_tile(hidden_width, feed)
        copies = [store.start(h2, h2_out), store.start(u, u_out), store.start(slope, slope_out)]
        got_down.wait()

        def down(at):
            e2[:, at] = x1[:, at] + (mm(u[...], down_w[:, at]) + vectors[6:7, at])

        each_tile(width, down)
        copies.append(store.start(e2, e2_out))
        norm_forward(e2, vectors[4:5, :], vectors[5:6, :], low)
        copies.append(store.start(low, low_out))
        wait_all(copies)

    @pl.when(jnp.logical_not(on_encoder))
    def _():
        got_down = load.start(down_in, down_w)
        got_first = load.start(first_in, first_w)
        got_cot = load.start(cot_in, cot)
        norm_forward(x1, vectors[2:3, :], vectors[3:4, :], h2)
        got_first.wait()

        def query(at):
            low[:, at] = mm(h2[...], first_w[:, at]).astype(bf16)

        each_tile(width, query)
        copies = [store.start(h2, hc_out), store.start(low, qc_out)]
        got_down.wait()
        got_cot.wait()

        def back(at):
            slope[:, at] = mm_nt(cot[...], down_w[at, :]).astype(bf16)

        each_tile(hidden_width, back)
        copies.append(store.start(slope, slope_out))
        wait_all(copies)

    wait_all(out_copies)


def cross_body(
    heads, flag, ids, vectors, in_bias, vec_in,
    memory_in, half_in, other_in, second_in, x1_in, qc_in, cot_in, ffn_in, h2_in, u_in, slope_in,
    vec_out, h2_out, u_out, slope_out, d2_out, grad_out, cc_out, dq_out, dk_out, dv_out, dm_out,
    memory, keys_w, values_w, second_w, x1, qc, cot, ffn_w, keys, values, weights, cc, d2, h2, u,
    slope, grad_normed, grad, grad_low, dq, dk, dv, dm, mask, gain_sum, offset_sum, loads, stores,
):
    width = memory.shape[1]
    hidden_width = ffn_w.shape[1]
    half = width // 2
    row_count, length = ids.shape[1], ids.shape[2]
    vec_out[...] = vec_in[...]

    @pl.when(flag[0] == 0)
    def _():
        load = Mover(loads)
        store = Mover(stores)
        core = flag[1]
        own_at = pl.ds(pl.multiple_of(core * half, half), half)
        other_at = pl.ds(pl.multiple_of((1 - core) * half, half), half)
        got_keys = [
            load.start(half_in.at[0], keys_w.at[own_at]),
            load.start(other_in.at[0], keys_w.at[other_at]),
            load.start(memory_in, memory),
        ]
        got_values = [
            load.start(half_in.at[1], values_w.at[own_at]),
            load.start(other_in.at[1], values_w.at[other_at]),
        ]
        got_query = load.start(qc_in, qc)
        got_second = [load.start(second_in, second_w), load.start(x1_in, x1)]
        got_ffn = [load.start(ffn_in, ffn_w), load.start(slope_in, slope)]
        got_cot = load.start(cot_in, cot)
        for row in range(row_count):
            mask[row] = jnp.where(
                same_sentence(ids[1:2, row, :], ids[0:1, row, :]), 0.0, masked_score
            )
        wait_all(got_keys)

        def project_keys(at):
            keys[:, at] = mm(memory[...], keys_w[:, at]).astype(bf16)

        each_tile(width, project_keys)
        wait_all(got_values)

        def project_values(at):
            values[:, at] = mm(memory[...], values_w[:, at]).astype(bf16)

        each_tile(width, project_values)
        got_query.wait()
        scale = (width // heads) ** (-0.5)

        @pl.loop(0, heads // 2)
        def _(pair):
            lanes = pl.ds(pl.multiple_of(pair * 128, 128), 128)
            for row in range(row_count):
                at = slice(row * length, (row + 1) * length)
                part, mixed = attend_pair(
                    qc[at, lanes], keys[at, lanes], values[at, lanes], [mask[row], mask[row]], scale
                )
                weights[row, pair] = part
                cc[at, lanes] = mixed.astype(bf16)

        copies = [store.start(cc, cc_out)]
        wait_all(got_second)

        def mix(at):
            d2[:, at] = x1[:, at] + mm(cc[...], second_w[:, at])

        each_tile(width, mix)
        copies.append(store.start(d2, d2_out))
        norm_forward(d2, vectors[4:5, :], vectors[5:6, :], h2)
        copies.append(store.start(h2, h2_out))
        wait_all(got_ffn)

        def feed(at):
            value, rate = gelu_parts(mm(h2[...], ffn_w[:, at]) + in_bias[:, at])
            u[:, at] = value.astype(bf16)
            slope[:, at] = (slope[:, at].astype(f32) * rate).astype(bf16)

        each_tile(hidden_width, feed)
        copies += [store.start(u, u_out), store.start(slope, slope_out)]

        def back(at):
            grad_normed[:, at] = mm_nt(slope[...], ffn_w[at, :])

        each_tile(width, back)
        got_cot.wait()
        norm_backward(d2, grad_normed, vectors[4:5, :], cot, grad, gain_sum, offset_sum)
        vec_out[4:5, :] = column_sum(gain_sum)
        vec_out[5:6, :] = column_sum(offset_sum)
        copies.append(store.start(grad, grad_out))

        def lower(at):
            grad_low[at, :] = grad[at, :].astype(bf16)

        each_rows(grad.shape[0], lower)

        def back_context(at):
            dm[:, at] = mm_nt(grad_low[...], second_w[at, :]).astype(bf16)

        each_tile(width, back_context)

        @pl.loop(0, heads // 2)
        def _(pair):
            lanes = pl.ds(pl.multiple_of(pair * 128, 128), 128)
            for row in range(row_count):
                at = slice(row * length, (row + 1) * length)
                grad_q, grad_k, grad_v, _ = attend_pair_back(
                    weights[row, pair], qc[at, lanes], keys[at, lanes], values[at, lanes],
                    dm[at, lanes], scale,
                )
                dq[at, lanes] = grad_q.astype(bf16)
                dk[at, lanes] = grad_k.astype(bf16)
                dv[at, lanes] = grad_v.astype(bf16)

        copies += [store.start(dq, dq_out), store.start(dk, dk_out), store.start(dv, dv_out)]

        def back_memory(at):
            dm[:, at] = (mm_nt(dk[...], keys_w[at, :]) + mm_nt(dv[...], values_w[at, :])).astype(bf16)

        each_tile(width, back_memory)
        copies.append(store.start(dm, dm_out))
        wait_all(copies)


def decoder_grads_body(
    flag, vectors, vec_in, fbias_in,
    u_in, slope_in, h2_in, cot_in, d2_in, down_in, cc_in, grad_in, hc_in, dq_in, memory_in, dk_in,
    dv_in, low_in,
    vec_out, fbias_out, low_out, down_out, ffn_out, cross_out,
    u, slope, h2, cot, d2, down_w, cc, grad, hc, dq, memory, dk, dv, low, down_g, ffn_g, cross_g,
    loads, stores,
):
    width = cot.shape[1]
    hidden_width = u.shape[1]
    vec_out[...] = vec_in[...]
    fbias_out[...] = fbias_in[...]

    @pl.when(flag[0] == 0)
    def _():
        load = Mover(loads)
        store = Mover(stores)
        got_down = [load.start(u_in, u), load.start(cot_in, cot)]
        got_ffn = [load.start(slope_in, slope), load.start(h2_in, h2)]
        got_cross = [
            load.start(hc_in, hc),
            load.start(dq_in, dq),
            load.start(cc_in, cc),
            load.start(grad_in, grad),
            load.start(memory_in, memory),
            load.start(dk_in, dk),
            load.start(dv_in, dv),
        ]
        got_out = [load.start(d2_in, d2), load.start(down_in, down_w)]
        wait_all(got_down)

        def down_grad(at):
            down_g[at, :] = mm_tn(u[:, at], cot[...]).astype(bf16)

        each_tile(hidden_width, down_grad)
        copies = [store.start(down_g, down_out)]
        vec_out[6:7, :] = jnp.sum(cot[...].astype(f32), axis=0, keepdims=True)
        wait_all(got_ffn)

        def ffn_grad(at):
            ffn_g[:, at] = mm_tn(h2[...], slope[:, at]).astype(bf16)
            fbias_out[:, at] = jnp.sum(slope[:, at].astype(f32), axis=0, keepdims=True)

        each_tile(hidden_width, ffn_grad)
        copies.append(store.start(ffn_g, ffn_out))
        wait_all(got_cross)

        def cross_grad(at):
            cross_g[0, :, at] = mm_tn(hc[...], dq[:, at]).astype(bf16)
            cross_g[1, :, at] = mm_tn(cc[...], grad[:, at].astype(bf16)).astype(bf16)
            cross_g[2, :, at] = mm_tn(memory[...], dk[:, at]).astype(bf16)
            cross_g[3, :, at] = mm_tn(memory[...], dv[:, at]).astype(bf16)

        each_tile(width, cross_grad)
        copies.append(store.start(cross_g, cross_out))
        wait_all(got_out)

        def down(at):
            value = d2[:, at] + (mm(u[...], down_w[:, at]) + vectors[6:7, at])
            low[:, at] = value.astype(bf16)

        each_tile(width, down)
        copies.append(store.start(low, low_out))
        wait_all(copies)


def encoder_down_body(
    flag, vectors, vec_in, dm_in, cot_in, e2_in, u_in, down_in,
    vec_out, grad_out, down_out,
    dm, cot, e2, u, grad, grad_low, down_g, gain_sum, offset_sum, loads, stores,
):
    hidden_width = u.shape[1]
    vec_out[...] = vec_in[...]

    @pl.when(flag[0] == 1)
    def _():
        load = Mover(loads)
        store = Mover(stores)
        got = [load.start(dm_in, dm), load.start(cot_in, cot), load.start(e2_in, e2)]
        got_u = load.start(u_in, u)
        wait_all(got)

        def total(at):
            grad[at, :] = dm[at, :].astype(f32) + cot[at, :].astype(f32)

        each_rows(grad.shape[0], total)
        norm_backward(e2, grad, vectors[4:5, :], None, grad, gain_sum, offset_sum)
        vec_out[4:5, :] = column_sum(gain_sum)
        vec_out[5:6, :] = column_sum(offset_sum)
        copies = [store.start(grad, grad_out)]

        def lower(at):
            grad_low[at, :] = grad[at, :].astype(bf16)

        each_rows(grad.shape[0], lower)
        vec_out[6:7, :] = jnp.sum(grad_low[...].astype(f32), axis=0, keepdims=True)
        got_u.wait()

        def down_grad(at):
            down_g[at, :] = mm_tn(u[:, at], grad_low[...]).astype(bf16)

        each_tile(hidden_width, down_grad)
        copies.append(store.start(down_g, down_out))
        wait_all(copies)


def encoder_ffn_body(
    flag, fbias_in, grad_in, down_in, slope_in, h2_in, ffn_old,
    fbias_out, slope_out, ffn_out,
    grad, grad_low, down_w, slope, h2, ffn_g, loads, stores,
):
    hidden_width = slope.shape[1]
    fbias_out[...] = fbias_in[...]

    @pl.when(flag[0] == 1)
    def _():
        load = Mover(loads)
        store = Mover(stores)
        got_grad = load.start(grad_in, grad)
        got = [load.start(down_in, down_w), load.start(slope_in, slope), load.start(h2_in, h2)]
        got_grad.wait()

        def lower(at):
            grad_low[at, :] = grad[at, :].astype(bf16)

        each_rows(grad.shape[0], lower)
        wait_all(got)

        def back(at):
            part = mm_nt(grad_low[...], down_w[at, :]) * slope[:, at].astype(f32)
            part = part.astype(bf16)
            slope[:, at] = part
            fbias_out[:, at] = jnp.sum(part.astype(f32), axis=0, keepdims=True)
            ffn_g[:, at] = mm_tn(h2[...], part).astype(bf16)

        each_tile(hidden_width, back)
        copies = [store.start(slope, slope_out), store.start(ffn_g, ffn_out)]
        wait_all(copies)


def tail_body(
    heads, wanted, flag, turned, vectors, vec_in, table_in,
    grad_in, part_in, matrix_in, x1_in, h1_in, qkv_in, weights_in, context_in, rows_in, qkvw_in,
    outw_in, result_in, out_old, qkv_old,
    vec_out, table_out, result_out, out_out, qkv_out,
    grad, part, matrix, x1, h1, qkv, weights, context, rows, qkv_w, out_w, grad_normed, grad_low,
    grad_context, grad_qkv, out_g, qkv_g, diagonals, gain_sum, offset_sum, loads, stores,
):
    width = x1.shape[1]
    row_count, length = weights.shape[0], weights.shape[2]
    vec_out[...] = vec_in[...]
    table_out[...] = table_in[...]

    @pl.when(flag[0] == wanted)
    def _():
        load = Mover(loads)
        store = Mover(stores)
        got_part = [load.start(part_in, part), load.start(matrix_in, matrix)]
        got_x1 = [load.start(x1_in, x1), load.start(grad_in, grad)]
        got_context = [load.start(context_in, context), load.start(outw_in, out_w)]
        got_attention = [load.start(weights_in, weights), load.start(qkv_in, qkv)]
        got_rest = [load.start(h1_in, h1), load.start(qkvw_in, qkv_w), load.start(rows_in, rows)]
        wait_all(got_part)

        def back(at):
            grad_normed[:, at] = mm_nt(part[...], matrix[at, :])

        each_tile(width, back)
        wait_all(got_x1)
        norm_backward(x1, grad_normed, vectors[2:3, :], grad, grad, gain_sum, offset_sum)
        vec_out[2:3, :] = column_sum(gain_sum)
        vec_out[3:4, :] = column_sum(offset_sum)

        def lower(at):
            grad_low[at, :] = grad[at, :].astype(bf16)

        each_rows(grad.shape[0], lower)
        wait_all(got_context)

        def back_out(at):
            grad_context[:, at] = mm_nt(grad_low[...], out_w[at, :]).astype(bf16)
            out_g[:, at] = mm_tn(context[...], grad_low[:, at]).astype(bf16)

        each_tile(width, back_out)
        copies = [store.start(out_g, out_out)]
        wait_all(got_attention)
        scale = (width // heads) ** (-0.5)

        @pl.loop(0, heads // 2)
        def _(pair):
            lanes = pl.multiple_of(pair * 128, 128)
            totals = [None, None]
            for row in range(row_count):
                at = slice(row * length, (row + 1) * length)
                grad_q, grad_k, grad_v, parts = attend_pair_back(
                    weights[row, pair],
                    qkv[at, pl.ds(lanes, 128)],
                    qkv[at, pl.ds(width + lanes, 128)],
                    qkv[at, pl.ds(2 * width + lanes, 128)],
                    grad_context[at, pl.ds(lanes, 128)],
                    scale,
                )
                grad_qkv[at, pl.ds(lanes, 128)] = grad_q.astype(bf16)
                grad_qkv[at, pl.ds(width + lanes, 128)] = grad_k.astype(bf16)
                grad_qkv[at, pl.ds(2 * width + lanes, 128)] = grad_v.astype(bf16)
                totals = [p if t is None else t + p for t, p in zip(totals, parts)]
            for head in range(2):
                padded = jnp.concatenate([totals[head], jnp.zeros((length, length), f32)], axis=1)
                folded = padded[0:8, :]
                for block in range(1, length // 8):
                    folded = folded + pltpu.roll(
                        padded[block * 8 : (block + 1) * 8, :], 2 * length - block * 8, 1
                    )
                line = folded[0:1, :]
                for sub in range(1, 8):
                    line = line + pltpu.roll(folded[sub : sub + 1, :], 2 * length - sub, 1)
                diagonals[pl.ds(pair * 2 + head, 1), :] = line

        one_hot = (
            turned[...] == lax.broadcasted_iota(jnp.int32, (table_out.shape[0], 2 * length), 0)
        ).astype(f32)
        table_out[...] = lax.dot_general(
            one_hot, diagonals[...], (((1,), (1,)), ((), ())), precision=lax.Precision.HIGHEST,
            preferred_element_type=f32,
        )
        wait_all(got_rest)

        def qkv_grad(at):
            qkv_g[:, at] = mm_tn(h1[...], grad_qkv[:, at]).astype(bf16)

        each_tile(3 * width, qkv_grad)
        copies.append(store.start(qkv_g, qkv_out))

        def back_normed(at):
            grad_normed[:, at] = mm_nt(grad_qkv[...], qkv_w[at, :])

        each_tile(width, back_normed)
        norm_backward(rows, grad_normed, vectors[0:1, :], grad, grad, gain_sum, offset_sum)
        vec_out[0:1, :] = column_sum(gain_sum)
        vec_out[1:2, :] = column_sum(offset_sum)
        copies.append(store.start(grad, result_out))
        wait_all(copies)


def shape_of(dims, dtype):
    return jax.ShapeDtypeStruct(tuple(dims), dtype)


def run_kernel(body, operands, places, outs, out_places, scratch, loads, stores, aliases, flops, name):
    return pl.pallas_call(
        body,
        in_specs=places,
        out_specs=out_places,
        out_shape=outs,
        scratch_shapes=[pltpu.VMEM(dims, dtype) for dims, dtype in scratch]
        + [pltpu.SemaphoreType.DMA((loads,)), pltpu.SemaphoreType.DMA((stores,))],
        input_output_aliases=aliases,
        compiler_params=pltpu.CompilerParams(vmem_limit_bytes=vmem_bytes),
        cost_estimate=pl.CostEstimate(flops=flops, bytes_accessed=flops // 400, transcendentals=0),
        name=name,
    )(*operands)


def scattered(total):
    low = lax.psum_scatter(total, "batch", scatter_dimension=0, tiled=True)
    return low.astype(f32)


def per_device(
    inputs, cotangent, segments, buckets, qkv_weight, out_weight, in_weight, down_weight,
    cross_first, cross_second, vectors, ffn_bias, position_table,
):
    row_count, length, width = inputs.shape[1:]
    heads = position_table.shape[2]
    bucket_count = position_table.shape[1]
    hidden = in_weight.shape[2]
    tokens = row_count * length
    pairs = heads // 2
    on_encoder = lax.axis_index("section") == 0
    place = lax.axis_index("batch")
    core = lax.rem(place, 2)
    devices = lax.axis_size("batch")
    flag = jnp.stack([on_encoder.astype(jnp.int32), core])
    turned = jnp.concatenate(
        [buckets[length - 1 :], jnp.full((1,), -1, jnp.int32), buckets[: length - 1]]
    )[None]
    rows = inputs.reshape(tokens, width)
    cot = cotangent.reshape(tokens, width)
    qkv_w, out_w, ffn_w, down_w = qkv_weight[0], out_weight[0], in_weight[0], down_weight[0]
    first_w, second_w = cross_first[0], cross_second[0]
    vec = jnp.concatenate([vectors[0], jnp.zeros((1, width), f32)])
    fbias = ffn_bias

    tw, th = (tokens, width), (tokens, hidden)
    wide = (tokens, 3 * width)
    square = (row_count, pairs, length, 2 * length)
    token_flops = 2 * tokens * width * width

    half = width // 2
    own_half = jnp.stack(
        [
            lax.dynamic_slice_in_dim(first_w, core * half, half),
            lax.dynamic_slice_in_dim(second_w, core * half, half),
        ]
    )
    half_sent = lax.ppermute(own_half, "section", [(0, 1)])
    half_other = lax.ppermute(half_sent, "batch", [(i, i ^ 1) for i in range(devices)])

    first_outs = [
        shape_of(tw, f32), shape_of(tw, bf16), shape_of(wide, bf16), shape_of(square, bf16),
        shape_of(tw, bf16), shape_of(tw, bf16), shape_of(th, bf16), shape_of(th, bf16),
        shape_of(tw, f32), shape_of(tw, bf16), shape_of(tw, bf16), shape_of(tw, bf16),
    ]
    x1, h1, qkv, weights, context, h2, u, slope, e2, low, hc, qc = run_kernel(
        functools.partial(first_body, heads),
        (flag, segments, turned, position_table[0], vec, fbias, rows, cot, qkv_w, out_w, ffn_w,
         down_w, first_w),
        [SMEM] + [VMEM] * 5 + [ANY] * 7,
        first_outs,
        [ANY] * 12,
        [
            (tw, bf16), ((width, 3 * width), bf16), ((width, width), bf16), ((width, hidden), bf16),
            ((hidden, width), bf16), ((width, width), bf16), (tw, bf16), (tw, bf16), (wide, bf16),
            (square, bf16), (tw, bf16), (tw, f32), (tw, bf16), (th, bf16), (th, bf16), (tw, f32),
            (tw, bf16), ((heads, 2 * length), f32), ((row_count, length, length), f32),
        ],
        8, 13, {}, 12 * token_flops, "first",
    )

    memory = lax.ppermute(low, "section", [(0, 1)])

    vec_grad = jnp.zeros((8, width), f32)
    fbias_grad = jnp.zeros((1, hidden), f32)
    table_grad = jnp.zeros((bucket_count, heads), f32)
    vec_grad, h2, u, slope, d2, grad, cc, dq, dk, dv, dm = run_kernel(
        functools.partial(cross_body, heads),
        (flag, segments, vec, fbias, vec_grad, memory, half_sent, half_other, second_w, x1, qc, cot,
         ffn_w, h2, u, slope),
        [SMEM] + [VMEM] * 4 + [ANY] * 11,
        [shape_of((8, width), f32), shape_of(tw, bf16), shape_of(th, bf16), shape_of(th, bf16),
         shape_of(tw, f32), shape_of(tw, f32)] + [shape_of(tw, bf16)] * 5,
        [VMEM] + [ANY] * 10,
        [
            (tw, bf16), ((width, width), bf16), ((width, width), bf16), ((width, width), bf16),
            (tw, f32), (tw, bf16), (tw, bf16), ((width, hidden), bf16), (tw, bf16), (tw, bf16),
            (square, bf16), (tw, bf16), (tw, f32), (tw, bf16), (th, bf16), (th, bf16), (tw, f32),
            (tw, f32), (tw, bf16), (tw, bf16), (tw, bf16), (tw, bf16), (tw, bf16),
            ((row_count, length, length), f32), ((8, width), f32), ((8, width), f32),
        ],
        11, 10, {4: 0, 13: 1, 14: 2, 15: 3}, 16 * token_flops, "cross",
    )

    returned = lax.ppermute(dm, "section", [(1, 0)])

    vec_grad, fbias_grad, low, down_g, ffn_g, cross_g = run_kernel(
        decoder_grads_body,
        (flag, vec, vec_grad, fbias_grad, u, slope, h2, cot, d2, down_w, cc, grad, hc, dq, memory,
         dk, dv, low),
        [SMEM] + [VMEM] * 3 + [ANY] * 14,
        [shape_of((8, width), f32), shape_of((1, hidden), f32), shape_of(tw, bf16),
         shape_of((hidden, width), bf16), shape_of((width, hidden), bf16),
         shape_of((4, width, width), bf16)],
        [VMEM, VMEM] + [ANY] * 4,
        [
            (th, bf16), (th, bf16), (tw, bf16), (tw, bf16), (tw, f32), ((hidden, width), bf16),
            (tw, bf16), (tw, f32), (tw, bf16), (tw, bf16), (tw, bf16), (tw, bf16), (tw, bf16),
            (tw, bf16), ((hidden, width), bf16), ((width, hidden), bf16),
            ((4, width, width), bf16),
        ],
        13, 4, {2: 0, 3: 1, 17: 2}, 16 * token_flops, "decoder_grads",
    )

    def tail(wanted, vec_grad, table_grad, grad, part, matrix, result, out_g, qkv_g, name):
        olds = () if result is None else (result, out_g, qkv_g)
        body = functools.partial(tail_body, heads, wanted)
        if result is None:

            def body(*refs):
                return tail_body(heads, wanted, *refs[:16], None, None, None, *refs[16:])

        depth = part.shape[1]
        return run_kernel(
            body,
            (flag, turned, vec, vec_grad, table_grad, grad, part, matrix, x1, h1, qkv, weights,
             context, rows, qkv_w, out_w) + olds,
            [SMEM] + [VMEM] * 4 + [ANY] * (11 + len(olds)),
            [shape_of((8, width), f32), shape_of((bucket_count, heads), f32), shape_of(tw, f32),
             shape_of((width, width), bf16), shape_of((width, 3 * width), bf16)],
            [VMEM, VMEM] + [ANY] * 3,
            [
                (tw, f32), ((tokens, depth), bf16), ((width, depth), bf16), (tw, f32), (tw, bf16),
                (wide, bf16), (square, bf16), (tw, bf16), (tw, bf16), ((width, 3 * width), bf16),
                ((width, width), bf16), (tw, f32), (tw, bf16), (tw, bf16), (wide, bf16),
                ((width, width), bf16), ((width, 3 * width), bf16), ((heads, 2 * length), f32),
                ((8, width), f32), ((8, width), f32),
            ],
            11, 3, {3: 0, 4: 1} | ({16: 2, 17: 3, 18: 4} if olds else {}), 16 * token_flops, name,
        )

    vec_grad, table_grad, result, out_g, qkv_g = tail(
        0, vec_grad, table_grad, grad, dq, first_w, None, None, None, "decoder_tail"
    )

    vec_grad, enc_grad, down_g = run_kernel(
        encoder_down_body,
        (flag, vec, vec_grad, returned, cot, e2, u, down_g),
        [SMEM] + [VMEM] * 2 + [ANY] * 5,
        [shape_of((8, width), f32), shape_of(tw, f32), shape_of((hidden, width), bf16)],
        [VMEM, ANY, ANY],
        [
            (tw, bf16), (tw, bf16), (tw, f32), (th, bf16), (tw, f32), (tw, bf16),
            ((hidden, width), bf16), ((8, width), f32), ((8, width), f32),
        ],
        4, 2, {2: 0, 7: 2}, 4 * token_flops, "encoder_down",
    )
    down_share = scattered(down_g)
    fbias_grad, slope, ffn_g = run_kernel(
        encoder_ffn_body,
        (flag, fbias_grad, enc_grad, down_w, slope, h2, ffn_g),
        [SMEM, VMEM] + [ANY] * 5,
        [shape_of((1, hidden), f32), shape_of(th, bf16), shape_of((width, hidden), bf16)],
        [VMEM, ANY, ANY],
        [
            (tw, f32), (tw, bf16), ((hidden, width), bf16), (th, bf16), (tw, bf16),
            ((width, hidden), bf16),
        ],
        4, 2, {1: 0, 4: 1, 6: 2}, 8 * token_flops, "encoder_ffn",
    )
    ffn_share = scattered(ffn_g)
    vec_grad, table_grad, result, out_g, qkv_g = tail(
        1, vec_grad, table_grad, enc_grad, slope, ffn_w, result, out_g, qkv_g, "encoder_tail"
    )
    out_share = scattered(out_g)
    qkv_share = scattered(qkv_g)
    cross_shares = lax.psum_scatter(cross_g, "batch", scatter_dimension=1, tiled=True)
    back_shares = lax.ppermute(cross_shares[2:], "section", [(1, 0)])
    cross_share = jnp.where(on_encoder, back_shares, cross_shares[:2]).astype(f32)
    vec_share = lax.psum_scatter(vec_grad[:7], "batch", scatter_dimension=1, tiled=True)
    fbias_share = lax.psum_scatter(fbias_grad, "batch", scatter_dimension=1, tiled=True)
    table_total = lax.psum(table_grad, "batch")
    return (
        low.reshape((1, row_count, length, width)),
        result.reshape((1, row_count, length, width)),
        qkv_share[None],
        out_share[None],
        ffn_share[None],
        down_share[None],
        cross_share[0][None],
        cross_share[1][None],
        vec_share[None],
        fbias_share,
        table_total[None],
    )


def solution(mesh):
    return jax.shard_map(
        per_device,
        mesh=mesh,
        in_specs=(
            P("section", "batch", None, None),
            P("section", "batch", None, None),
            P(None, "batch", None),
            P(),
            P("section", None, None),
            P("section", None, None),
            P("section", None, None),
            P("section", None, None),
            P("section", None, None),
            P("section", None, None),
            P("section", None, None),
            P("section", None),
            P("section", None, None),
        ),
        out_specs=(
            P("section", "batch", None, None),
            P("section", "batch", None, None),
            P("section", "batch", None),
            P("section", "batch", None),
            P("section", "batch", None),
            P("section", "batch", None),
            P("section", "batch", None),
            P("section", "batch", None),
            P("section", None, "batch"),
            P("section", "batch"),
            P("section", None, None),
        ),
        check_vma=False,
    )
```

time: 1600 us -> 680 us (0.42)
  local copies, waits for them, and re-layouts: 630 us -> 15.2 us
  matrix products: 240 us -> 0 us
  other arithmetic: 152 us -> 9.19 us
  Pallas kernels: 0 us -> 98.3 us
    gather x2 -> x0, local copies, waits for them, and re-layouts: 409 us -> none  [per_device(): buckets[offsets][:, :, None] == jnp.arange(bucket_count)[None, None, :]]
    dot_general x53 -> x0, matrix products: 229 us -> none  [the longest x12 54.5 us: weight_grad(): jnp.einsum('rsd,rse->de', left_side, grad_side, preferred_element_type=jn...]
    pallas_call x0 -> x7, Pallas kernels: none -> 98.3 us  [run_kernel(): pl.pallas_call(body, in_specs=places, out_specs=out_places, out_shape=out...]
    another operation x52 -> x0, local copies, waits for them, and re-layouts: 93.7 us -> none
    add x18 -> x0, other arithmetic: 84.5 us -> none  [the longest x8 66.5 us: per_device(): jax.tree.map(jnp.add, finish_summed, micro_grads)]
    cond x132 -> x0, local copies, waits for them, and re-layouts: 82.8 us -> none  [the longest x8 60.2 us: run_backward(): lax.cond(on_encoder, encode_back, spare_branch(encode_back), cotangent_pa...]
    psum x0 -> x1, blocking collectives: none -> 60.9 us  [per_device(): table_total = lax.psum(table_grad, 'batch')]
    unnamed x1 -> x0, blocking collectives: 60.5 us -> none
  transfers between devices with their start and end apart: 15 -> 12, of which waited for: 9 -> 9; matrix products, arithmetic and copies ran while one was open for 25% -> 2% of each run, Pallas kernels for 0% -> 9%
where the time goes in v2:
time: 680 us; the launch traced here: 679 us
  waiting for transfers between devices  472 us (69%)
  Pallas kernels  98.3 us (14%)
  blocking collectives  60.9 us (9%)
  local copies, waits for them, and re-layouts  15.2 us (2%)
  between operations  14.3 us (2%)
  other arithmetic  9.19 us (1%)
  starting transfers between devices  9.14 us (1%)
    reduce_scatter x4, waiting for transfers between devices, scattered(): low = lax.psum_scatter(total, 'batch', scatter_dimension=0, tiled=True)  280 us
    pallas_call x7, Pallas kernels, run_kernel(): pl.pallas_call(body, in_specs=places, out_specs=out_places, out_shape=out...  98.3 us
    reduce_scatter x1, waiting for transfers between devices, per_device(): lax.psum_scatter(cross_g, 'batch', scatter_dimension=1, tiled=True)  76.7 us
    psum x1, blocking collectives, per_device(): table_total = lax.psum(table_grad, 'batch')  60.9 us
    ppermute x1, waiting for transfers between devices, per_device(): returned = lax.ppermute(dm, 'section', [(1, 0)])  50.4 us
    unnamed x9, waiting for transfers between devices  24.3 us
    ppermute x1, waiting for transfers between devices, per_device(): half_sent = lax.ppermute(own_half, 'section', [(0, 1)])  22.5 us
    ppermute x1, waiting for transfers between devices, per_device(): memory = lax.ppermute(low, 'section', [(0, 1)])  17.9 us
  transfers between devices with their start and end apart: 12, of which 9 were waited for; matrix products, arithmetic and copies ran while one was open for 2% of the time, Pallas kernels for 9%

profile of v2, /device:TPU:0, one launch (start us, length us, event | category | flops | bytes accessed | tf_op | source)
XLA Modules:
  0.0 679.2 jit_solution(10614274090080223913)
XLA Ops:
  7.2 0.0 copy-start.1
  7.2 0.0 reduce-scatter.24.cloned.1.call-start
  7.2 1.2 constant_dynamic-slice_fusion
  8.4 0.2 copy-done.1
  8.7 0.1 pad_maximum_fusion
  8.8 4.9 collective-permute-start.1
  13.8 0.1 slice.21
  13.9 0.7 copy.49
  14.6 0.6 concatenate.6.vectors.refs_2_
  15.2 0.6 pad_add_fusion.1.flag.refs_0_
  15.8 0.7 pad_add_fusion
  16.4 22.5 %collective-permute-done.1.half_in = bf16[2,384,768]{2,1,0:T(8,128)(2,1)S(1)} collective-permute-done((bf16[2,384,768]{2,1,0:T(8,128)(2,1)S(1)}, bf16[2,384,768]{2,1,0:T(8,128)(2,1)S(1)}, u32[]{:S(2)}, u32[]{:S(2)}) %collective-permute-start.1) | collective-permute-done | bytes 1179680 | tf_op jit(solution)/shard_map/ppermute | solution.py:723
  38.9 29.5 %first.1 = (f32[512,768]{1,0:T(8,128)}, bf16[512,768]{1,0:T(8,128)(2,1)}, bf16[512,2304]{1,0:T(8,128)(2,1)}, bf16[2,6,256,512]{3,2,1,0:T(8,128)(2,1)}, bf16[512,...) custom-call(s32[2]{0:T(128)} %pad_add_fusion.1.flag.refs_0_, ...), custom_call_target="tpu_custom_call" | custom-call | flops 7247757312 | bytes 18119392 | tf_op jit(solution)/shard_map/first/pallas_call | solution.py:667
  68.5 1.3 collective-permute-start
  69.8 17.9 %collective-permute-done.memory_in = bf16[512,768]{1,0:T(8,128)(2,1)S(1)} collective-permute-done((bf16[512,768]{1,0:T(8,128)(2,1)}, bf16[512,768]{1,0:T(8,128)(2,1)S(1)}, u32[]{:S(2)}, u32[]{:S(2)}) %collective-permute-start) | collective-permute-done | bytes 786464 | tf_op jit(solution)/shard_map/ppermute | solution.py:747
  87.7 0.0 collective-permute-done.2.other_in
  87.7 0.7 broadcast_in_dim.43.vec_in
  88.3 0.3 copy-done.7
  88.6 1.6 cross.1
  90.2 1.3 collective-permute-start.3
  91.5 0.6 broadcast_in_dim.45.fbias_in
  92.1 1.8 decoder_grads.1
  93.9 0.6 broadcast_in_dim.46.clone.refs_4_
  94.5 1.6 decoder_tail.1
  96.0 50.4 %collective-permute-done.3.dm_in = bf16[512,768]{1,0:T(8,128)(2,1)S(1)} collective-permute-done((bf16[512,768]{1,0:T(8,128)(2,1)}, bf16[512,768]{1,0:T(8,128)(2,1)S(1)}, u32[]{:S(2)}, u32[]{:S(2)}) %collective-permute-start.3) | collective-permute-done | bytes 786464 | tf_op jit(solution)/shard_map/ppermute | solution.py:770
  146.4 0.9 copy-done
  147.3 13.6 %encoder_down.1 = (f32[8,768]{1,0:T(8,128)}, f32[512,768]{1,0:T(8,128)}, bf16[3072,768]{1,0:T(8,128)(2,1)}) custom-call(s32[2]{0:T(128)} %pad_add_fusion.1.flag.refs_0_, f32[8,768]{1,0:T(8,128)} %concatenate.6.vectors.refs_2_, f32[8,768]{1,0:T(8,128)} %get-tuple-element.79.vec_in, ...), custom_call_target="tpu_custom_call", output_to_operand_aliasing={{0}: (2, {}), {2}: (7, {})} | custom-call | flops 2415919104 | bytes 6039797 | tf_op jit(solution)/shard_map/encoder_down/pallas_call | solution.py:667
  160.9 20.6 %encoder_ffn.1 = (f32[1,3072]{1,0:T(1,128)}, bf16[512,3072]{1,0:T(8,128)(2,1)}, bf16[768,3072]{1,0:T(8,128)(2,1)}) custom-call(s32[2]{0:T(128)} %pad_add_fusion.1.flag.refs_0_, f32[1,3072]{1,0:T(1,128)} %get-tuple-element.86.fbias_in, f32[512,768]{1,0:T(8,128)} %get-tuple-element.85.grad_in, ...), custom_call_target="tpu_custom_call", output_to_operand_aliasing={{0}: (1, {}), {1}: (4, {}), {2}: (6, {})} | custom-call | flops 4831838208 | bytes 12079595 | tf_op jit(solution)/shard_map/encoder_ffn/pallas_call | solution.py:667
  181.5 2.4 copy.55
  183.9 0.0 reduce-scatter.24.cloned.1.call-update
  184.0 0.0 reduce-scatter.22.cloned.1.call-start
  184.0 29.7 %encoder_tail.1 = (f32[8,768]{1,0:T(8,128)}, f32[32,12]{1,0:T(8,128)}, f32[512,768]{1,0:T(8,128)}, bf16[768,768]{1,0:T(8,128)(2,1)}, bf16[768,2304]{1,0:T(8,128)(2,1)}) custom-call(s32[2]{0:T(128)} %pad_add_fusion.1.flag.refs_0_, s32[1,512]{1,0:T(1,128)} %bitcast.54, ...), custom_call_target="tpu_custom_call", output_to_operand_aliasing={{0}: (3, {}), {1}: (4, {}), {2}: (16, {}), {3}: (17, {}), {... | custom-call | flops 9663676416 | bytes 24159192 | tf_op jit(solution)/shard_map/encoder_tail/pallas_call | solution.py:667
  213.7 1.7 copy.53
  215.4 0.0 reduce-scatter.22.cloned.1.call-update
  215.4 0.0 reduce-scatter.14.cloned.1.call-start
  215.5 0.7 reduce-scatter.14.cloned.1.call-update
  216.1 0.0 reduce-scatter.20.cloned.1.call-start
  216.2 0.5 reduce-scatter.20.cloned.1.call-update
  216.7 0.0 reduce-scatter.12.cloned.1.call-start
  216.8 0.5 reduce-scatter.12.cloned.1.call-update
  217.3 0.0 reduce-scatter.16.cloned.1.call-start
  217.4 0.5 reduce-scatter.16.cloned.1.call-update
  217.9 0.0 reduce-scatter.18.cloned.1.call-start
  217.9 0.0 copy-start.2
  217.9 0.7 reduce-scatter.18.cloned.1.call-update
  218.6 0.0 copy-done.2
  218.7 60.9 %psum.7 = f32[1,32,12]{2,1,0:T(8,128)S(1)} all-reduce(f32[1,32,12]{2,1,0:T(8,128)S(1)} %bitcast.49), channel_id=1, replica_groups=mesh['section'=2,'batch'=16] {'batch'}, use_global_device_ids=true, to_apply=%region_7.8 | all-reduce | flops 384 | bytes 3072 | tf_op jit(solution)/shard_map/psum | solution.py:857
  279.5 0.7 copy.52
  280.2 1.5 copy.56
  281.7 21.3 %reduce-scatter.22.cloned.1.call-done = f32[48,7]{1,0:T(8,128)} async-done(((f32[768,7]{1,0:T(8,128)}), f32[48,7]{1,0:T(8,128)}) %reduce-scatter.22.cloned.1.call-update) | async-done | bytes 1360
  303.1 1.4 copy.51
  304.5 59.3 %reduce-scatter.14.cloned.1.call-done = bf16[48,768]{1,0:T(8,128)(2,1)} async-done(((bf16[768,768]{1,0:T(8,128)(2,1)}), bf16[48,768]{1,0:T(8,128)(2,1)}) %reduce-scatter.14.cloned.1.call-update) | async-done | bytes 73744 | tf_op jit(solution)/shard_map/reduce_scatter | solution.py:682
  363.8 1.6 bitcast_convert_fusion.3
  365.4 76.7 %reduce-scatter.20.cloned.1.call-done = bf16[4,48,768]{2,1,0:T(8,128)(2,1)} async-done(((bf16[4,768,768]{2,1,0:T(8,128)(2,1)}), bf16[4,48,768]{2,1,0:T(8,128)(2,1)}) %reduce-scatter.20.cloned.1.call-update) | async-done | bytes 294928 | tf_op jit(solution)/shard_map/reduce_scatter | solution.py:852
  442.1 0.9 slice.28
  443.0 1.3 collective-permute-start.4
  444.3 69.1 %reduce-scatter.12.cloned.1.call-done = bf16[48,2304]{1,0:T(8,128)(2,1)} async-done(((bf16[768,2304]{1,0:T(8,128)(2,1)}), bf16[48,2304]{1,0:T(8,128)(2,1)}) %reduce-scatter.12.cloned.1.call-update) | async-done | bytes 221200 | tf_op jit(solution)/shard_map/reduce_scatter | solution.py:682
  513.3 1.7 bitcast_convert_fusion.2
  515.1 0.9 fusion
  516.0 0.7 fusion.1
  516.7 75.3 %reduce-scatter.16.cloned.1.call-done = bf16[48,3072]{1,0:T(8,128)(2,1)} async-done(((bf16[768,3072]{1,0:T(8,128)(2,1)}), bf16[48,3072]{1,0:T(8,128)(2,1)}) %reduce-scatter.16.cloned.1.call-update) | async-done | bytes 294928 | tf_op jit(solution)/shard_map/reduce_scatter | solution.py:682
  592.1 1.8 bitcast_convert_fusion.1
  593.9 76.7 %reduce-scatter.18.cloned.1.call-done = bf16[192,768]{1,0:T(8,128)(2,1)} async-done(((bf16[3072,768]{1,0:T(8,128)(2,1)}), bf16[192,768]{1,0:T(8,128)(2,1)}) %reduce-scatter.18.cloned.1.call-update) | async-done | bytes 294928 | tf_op jit(solution)/shard_map/reduce_scatter | solution.py:682
  670.5 1.8 bitcast_convert_fusion
  (17 shorter events, 0.1 us)
Async XLA Ops:
  7.2 1.5 copy-start.1
  7.2 273.0 %reduce-scatter.24.cloned.1.call-start = ((), (), s32[]{:S(2)}) async-start(), calls=%async_computation.13 | async-start | bytes 1671168
  8.6 5.1 copy-start.5
  8.6 5.2 copy-start.3
  8.6 5.2 copy-start.4
  8.6 7.1 %slice-start = ((s32[511]{0:T(512)}), s32[255]{0:T(256)S(1)}, s32[]{:S(2)}) async-start(s32[511]{0:T(512)} %param.16), calls=%async_computation.14 | async-start | bytes 2048 | tf_op jit(solution)/shard_map/slice | solution.py:702
  8.8 30.1 %collective-permute-start.1 = (bf16[2,384,768]{2,1,0:T(8,128)(2,1)S(1)}, bf16[2,384,768]{2,1,0:T(8,128)(2,1)S(1)}, u32[]{:S(2)}, u32[]{:S(2)}) collective-permute-start(bf16[2,384,768]{2,1,0:T(8,128)(2,1)S(1)} %pad_maximum_fusion), channel_id=1, source_target_pairs={{0,16},{1,17},{2,18},{3,19},{4,20},{5,21},{6,22},{7,23},{8,24},{9,... | collective-permute-start | bytes 3538952 | tf_op jit(solution)/shard_map/ppermute | solution.py:723
  38.9 29.6 %copy-start.6 = (bf16[2,384,768]{2,1,0:T(8,128)(2,1)}, bf16[2,384,768]{2,1,0:T(8,128)(2,1)S(1)}, u32[]{:S(2)}) copy-start(bf16[2,384,768]{2,1,0:T(8,128)(2,1)S(1)} %collective-permute-done.1.half_in) | copy-start | bytes 3538948
  38.9 48.8 %collective-permute-start.2 = (bf16[2,384,768]{2,1,0:T(8,128)(2,1)S(1)}, bf16[2,384,768]{2,1,0:T(8,128)(2,1)}, u32[]{:S(2)}, u32[]{:S(2)}) collective-permute-start(bf16[2,384,768]{2,1,0:T(8,128)(2,1)S(1)} %collective-permute-done.1.half_in), channel_id=1, source_target_pairs={{0,1},{1,0},{2,3},{3,2},{4,5},{5,4},{6,7},{7,6},{8,9},{9,8},{10,11... | collective-permute-start | bytes 3538952 | tf_op jit(solution)/shard_map/ppermute | solution.py:724
  68.5 19.2 %collective-permute-start = (bf16[512,768]{1,0:T(8,128)(2,1)}, bf16[512,768]{1,0:T(8,128)(2,1)S(1)}, u32[]{:S(2)}, u32[]{:S(2)}) collective-permute-start(bf16[512,768]{1,0:T(8,128)(2,1)} %get-tuple-element.56.low_in), channel_id=1, source_target_pairs={{0,16},{1,17},{2,18},{3,19},{4,20},{5,21},{6,22},{7,23},{8,24},{9,... | collective-permute-start | bytes 2359304 | tf_op jit(solution)/shard_map/ppermute | solution.py:747
  87.7 0.9 copy-start.7
  90.2 56.3 %collective-permute-start.3 = (bf16[512,768]{1,0:T(8,128)(2,1)}, bf16[512,768]{1,0:T(8,128)(2,1)S(1)}, u32[]{:S(2)}, u32[]{:S(2)}) collective-permute-start(bf16[512,768]{1,0:T(8,128)(2,1)} %get-tuple-element.80), channel_id=1, source_target_pairs={{16,0},{17,1},{18,2},{19,3},{20,4},{21,5},{22,6},{23,7},{24,8},{25... | collective-permute-start | bytes 2359304 | tf_op jit(solution)/shard_map/ppermute | solution.py:770
  146.4 0.9 copy-start
  184.0 119.1 %reduce-scatter.22.cloned.1.call-start = ((), (), s32[]{:S(2)}) async-start(), calls=%async_computation.12 | async-start | bytes 417792
  215.4 148.4 %reduce-scatter.14.cloned.1.call-start = ((), (), s32[]{:S(2)}) async-start(), calls=%async_computation.8 | async-start | bytes 1253376 | tf_op jit(solution)/shard_map/reduce_scatter | solution.py:682
  216.1 225.9 %reduce-scatter.20.cloned.1.call-start = ((), (), s32[]{:S(2)}) async-start(), calls=%async_computation.11 | async-start | bytes 5013504 | tf_op jit(solution)/shard_map/reduce_scatter | solution.py:852
  216.7 296.6 %reduce-scatter.12.cloned.1.call-start = ((), (), s32[]{:S(2)}) async-start(), calls=%async_computation.7 | async-start | bytes 3760128 | tf_op jit(solution)/shard_map/reduce_scatter | solution.py:682
  217.3 374.8 %reduce-scatter.16.cloned.1.call-start = ((), (), s32[]{:S(2)}) async-start(), calls=%async_computation.9 | async-start | bytes 5013504 | tf_op jit(solution)/shard_map/reduce_scatter | solution.py:682
  217.9 452.7 %reduce-scatter.18.cloned.1.call-start = ((), (), s32[]{:S(2)}) async-start(), calls=%async_computation.10 | async-start | bytes 5013504 | tf_op jit(solution)/shard_map/reduce_scatter | solution.py:682
  217.9 0.7 copy-start.2
  443.0 72.1 %collective-permute-start.4 = (bf16[2,48,768]{2,1,0:T(8,128)(2,1)S(1)}, bf16[2,48,768]{2,1,0:T(8,128)(2,1)S(1)}, u32[]{:S(2)}, u32[]{:S(2)}) collective-permute-start(bf16[2,48,768]{2,1,0:T(8,128)(2,1)S(1)} %slice.28), channel_id=1, source_target_pairs={{16,0},{17,1},{18,2},{19,3},{20,4},{21,5},{22,6},{23,7},{24,8},{25... | collective-permute-start | bytes 442376 | tf_op jit(solution)/shard_map/ppermute | solution.py:853
Sparse Core Ops, SparseCore 0:
  184.1 59.7 reduce-scatter.23
  248.4 54.6 reduce-scatter.21
  306.7 57.0 reduce-scatter.13
  367.5 74.4 reduce-scatter.19
  446.3 67.0 reduce-scatter.11
  517.5 74.4 reduce-scatter.15
  595.9 74.5 reduce-scatter.17
